TPU v7x, 128 devices: a whole 4x4x4 slice. The times are simulated.
128 devices in a mesh: px: 16 (over z_hi, x, core), py: 8 (over z_lo, y).
Axes of the slice: x: 4, y: 4, z: 4 (z_hi: 2, z_lo: 2; z = z_hi * 2 + z_lo), core: 2. Of those that a mesh axis runs over, the one named last changes fastest.
Arguments:
- cotangent: float32 [128, 128, 128], P('px', 'py'), may hold values from -6 to 6
- fraction: float32 [3, 128, 128, 128], P(None, 'px', 'py'), may hold values from 0 to 0.999
- grid_base: int32 [3, 128, 128, 128], P(None, 'px', 'py'), may hold values from 0 to 511, as said below
- cell_count: int32 [128, 128], P('px', 'py'), may hold values from 32 to 128, as said below
- influence: float32 [256, 512, 512], P(('px', 'py')), as said below
Outputs:
- charge_gradient: float32 [128, 128, 128], P('px', 'py')
Inputs may be any that keep to these rules, and one draw needn't show every extreme that they name: grid_base[0] // 4 is the cell's first index and grid_base[1] // 4 its second; grid_base[2] lies in 0 to 255. `cell_count`: some cell is full. Positive and even: influence[kz, kx, ky] equals influence[-kz, -kx, -ky], wave numbers taken modulo 256, 512, 512.
All inputs are finite; a program needn't handle non-finite values.
Results may differ from a plain program's by a relative error of at most 0.0003.
Values sent between devices are 32-bit elements; how exact they have to be, the bound alone decides.
No kernel may reach another device: no remote copies, remote signals or barrier semaphores. Data moves between devices by JAX's collectives and lax.ppermute only.
A program may use at most 128 MiB of HBM per device.

v0:
```python
import math

import jax
import jax.numpy as jnp
from jax import lax
from jax.sharding import PartitionSpec as P

NZ = 256
CELL = 4


exact_prec = lax.Precision.HIGHEST


def with_halo(block, sides, width):
    for axis, dim in sides:
        count = lax.axis_size(axis)
        forward = [(i, i + 1) for i in range(count - 1)]
        forward.append((count - 1, 0))
        backward = [(target, source) for source, target in forward]
        low = lax.ppermute(
            lax.slice_in_dim(block, block.shape[dim] - width, None, axis=dim), axis, forward
        )
        high = lax.ppermute(lax.slice_in_dim(block, 0, width, axis=dim), axis, backward)
        block = jnp.concatenate([low, block, high], axis=dim)
    return block


def spline_weights(fractions):
    nothing = jnp.zeros_like(fractions)
    values = [fractions, 1.0 - fractions]
    for degree in (3, 4, 5):
        updated = []
        for position in range(degree):
            upper_term = values[position] if position < degree - 1 else nothing
            lower_term = values[position - 1] if position >= 1 else nothing
            updated.append(
                ((fractions + position) * upper_term + (degree - fractions - position) * lower_term)
                / (degree - 1)
            )
        values = updated
    return jnp.stack(values)


def window_weights(offsets, weights):
    position = jnp.arange(8, dtype=jnp.int32)[:, None]
    selected = 4 + offsets[:, :, None, :] - position
    summed = jnp.zeros(selected.shape, jnp.float32)
    for degree in range(5):
        summed = summed + jnp.where(selected == degree, weights[degree][:, :, None, :], 0.0)
    return summed


def depth_weights(depth_base, weights):
    levels = jnp.arange(NZ, dtype=jnp.int32)[None, :, None]
    offsets = (levels - depth_base[:, None, :] + NZ // 2) % NZ - NZ // 2
    selected = 2 - offsets
    summed = jnp.zeros(selected.shape, jnp.float32)
    for degree in range(5):
        summed = summed + jnp.where(selected == degree, weights[degree][:, None, :], 0.0)
    return summed


def fold_rims(mesh_grid, axis_index):
    extent = mesh_grid.shape[axis_index]
    interior = lax.slice_in_dim(mesh_grid, 4, extent - 4, axis=axis_index)
    interior_size = extent - 8
    lower_rim = lax.slice_in_dim(mesh_grid, 0, 2, axis=axis_index)
    upper_rim = lax.slice_in_dim(mesh_grid, extent - 2, extent, axis=axis_index)
    return jnp.concatenate(
        [
            lax.slice_in_dim(interior, 0, 2, axis=axis_index) + lower_rim,
            lax.slice_in_dim(interior, 2, interior_size - 2, axis=axis_index),
            lax.slice_in_dim(interior, interior_size - 2, interior_size, axis=axis_index)
            + upper_rim,
        ],
        axis=axis_index,
    )


def cosine_sine(length):
    indices = jnp.arange(length, dtype=jnp.int32)
    phases = indices[:, None] * indices[None, :] % length
    angles = phases.astype(jnp.float32) * (2.0 * math.pi / length)
    return (jnp.cos(angles), jnp.sin(angles))


def complex_table(length, sign):
    cosine, sine_part = cosine_sine(length)
    turned = sign * sine_part
    return jnp.stack([jnp.stack([cosine, turned]), jnp.stack([-turned, cosine])])


def per_device(cotangent, fraction, grid_base, cell_count, influence):
    cells_x, cells_y, slot_count = cotangent.shape
    local_x = cells_x * CELL
    local_y = cells_y * CELL
    slot_ids = jnp.arange(slot_count, dtype=jnp.int32)
    occupied = slot_ids[None, None, :] < cell_count[:, :, None]
    charge = jnp.where(occupied, cotangent, jnp.zeros_like(cotangent))
    window_x = window_weights(grid_base[0] % CELL, spline_weights(fraction[0]))
    window_y = window_weights(grid_base[1] % CELL, spline_weights(fraction[1]))
    depth_rows = jnp.moveaxis(spline_weights(fraction[2]), 1, 0)

    def spread_row(row):
        charge_row, across_x, across_y, across_z, base_z = row
        depth_table_row = depth_weights(base_z, across_z)
        lifted = charge_row[:, None, None, :] * across_x[:, :, None, :] * across_y[:, None, :, :]
        patches = jnp.einsum("buvs,bzs->buvz", lifted, depth_table_row, precision=exact_prec)
        stripe = jnp.zeros((8, local_y + 4, NZ), jnp.float32)
        for which_half in (0, 1):
            quarter = patches[:, :, CELL * which_half : CELL * which_half + CELL]
            quarter = jnp.transpose(quarter, (1, 0, 2, 3))
            quarter = jnp.pad(quarter, ((0, 0), (which_half, 1 - which_half), (0, 0), (0, 0)))
            stripe = stripe + quarter.reshape(8, local_y + 4, NZ)
        return stripe

    stripes = lax.map(spread_row, (charge, window_x, window_y, depth_rows, grid_base[2]))
    upper_half = jnp.pad(stripes[:, :CELL], ((0, 1), (0, 0), (0, 0), (0, 0)))
    lower_half = jnp.pad(stripes[:, CELL:], ((1, 0), (0, 0), (0, 0), (0, 0)))
    extended = (upper_half + lower_half).reshape(local_x + 4, local_y + 4, NZ)
    with_rims = with_halo(extended, (("px", 0), ("py", 1)), 2)
    spread = fold_rims(fold_rims(with_rims, 0), 1)
    px_size = lax.axis_size("px")
    py_size = lax.axis_size("py")
    full_x = px_size * local_x
    full_y = py_size * local_y
    cosine_z, sine_z = cosine_sine(NZ)
    depth_table = jnp.stack([cosine_z, -sine_z])
    forward_z, inverse_z = (depth_table, depth_table)
    spectrum_z = jnp.einsum("xyz,ckz->ckxy", spread, forward_z, precision=exact_prec)
    forward_y = complex_table(full_y, 1.0)
    forward_x = complex_table(full_x, 1.0)
    inverse_y = complex_table(full_y, -1.0)
    inverse_x = complex_table(full_x, -1.0)
    mixed_grid = lax.all_to_all(
        lax.all_to_all(spectrum_z, "px", split_axis=1, concat_axis=2, tiled=True),
        "py",
        split_axis=1,
        concat_axis=3,
        tiled=True,
    )
    along_y = jnp.einsum("czxy,dcyk->dzxk", mixed_grid, forward_y, precision=exact_prec)
    full_spectrum = jnp.einsum("czxy,dcxk->dzky", along_y, forward_x, precision=exact_prec)
    scaled = full_spectrum * influence[None]
    back_y = jnp.einsum("czxy,dcyk->dzxk", scaled, inverse_y, precision=exact_prec)
    back_x = jnp.einsum("czxy,dcxk->dzky", back_y, inverse_x, precision=exact_prec)
    half_back = lax.all_to_all(back_x, "py", split_axis=3, concat_axis=1, tiled=True)
    returned = lax.all_to_all(half_back, "px", split_axis=2, concat_axis=1, tiled=True)
    potential = jnp.einsum("ckxy,ckz->xyz", returned, inverse_z, precision=exact_prec) * (
        1.0 / (NZ * full_x * full_y)
    )
    halo_potential = with_halo(potential, (("px", 0), ("py", 1)), 2)

    def gather_row(row):
        row_index, across_x, across_y, across_z, base_z = row
        depth_table_row = depth_weights(base_z, across_z)
        stripe = lax.dynamic_slice_in_dim(halo_potential, row_index * CELL, 8, 0)
        blocks = stripe.reshape(8, cells_y + 1, CELL, NZ)
        window = jnp.concatenate([blocks[:, :-1], blocks[:, 1:]], axis=2)
        partial_value = jnp.einsum("ubvz,bzs->buvs", window, depth_table_row, precision=exact_prec)
        return jnp.sum(
            partial_value * across_x[:, :, None, :] * across_y[:, None, :, :], axis=(1, 2)
        )

    row_ids = jnp.arange(cells_x, dtype=jnp.int32)
    gradient = lax.map(gather_row, (row_ids, window_x, window_y, depth_rows, grid_base[2]))
    return jnp.where(occupied, gradient, jnp.zeros_like(gradient))


def solution(mesh):
    placed = (
        P("px", "py", None),
        P(None, "px", "py", None),
        P(None, "px", "py", None),
        P("px", "py"),
        P(("px", "py"), None, None),
    )
    return jax.shard_map(
        per_device, mesh=mesh, in_specs=placed, out_specs=P("px", "py", None), check_vma=False
    )
```

profile of v0, /device:TPU:0, one launch (start us, length us, event | category | flops | bytes accessed | tf_op | source)
XLA Modules:
  0.0 597.5 jit_solution(4433821049493570981)
XLA Ops:
  8.9 45.9 %while.26 = (s32[]{:T(128)}, f32[8,8,68,256]{3,1,2,0:T(8,128)}, f32[8,16,128]{2,1,0:T(8,128)S(1)}, f32[8,16,8,128]{3,2,1,0:T(8,128)S(1)}, f32[8,16,8,128]{3,2,1,...) while((s32[]{:T(128)}, f32[8,8,68,256]{3,1,2,0:T(8,128)}, ...), condition=%wide.region_1.2_spmd.clone, body=%wide.region_0.1_spmd.sunk.clone | while | flops 418144256 | bytes 7545505 | solution.py:118
  9.0 4.2 fusion.261
  14.7 4.2 fusion.261
  20.5 4.2 fusion.261
  26.2 4.2 fusion.261
  32.0 4.2 fusion.261
  37.7 4.2 fusion.261
  43.4 4.2 fusion.261
  49.2 4.2 fusion.261
  54.8 4.6 fusion.241
  60.6 5.7 collective-permute-start.1
  76.8 5.5 fusion.141
  82.3 9.2 %copy.49 = f32[2,256,32,64]{3,2,0,1:T(8,128)} copy(f32[2,256,32,64]{1,3,2,0:T(8,128)} %fusion.141) | data formatting | bytes 8388608 | tf_op jit(solution)/shard_map/xyz,ckz->ckxy/dot_general | solution.py:131
  91.5 13.3 %reshape.686 = f32[16,1,65536]{2,1,0:T(1,128)} reshape(f32[256,2,32,64]{3,2,1,0:T(8,128)} %bitcast.527) | data formatting | bytes 8388608
  104.8 58.3 %all_to_all.72 = f32[16,1,65536]{2,1,0:T(1,128)} all-to-all(f32[16,1,65536]{2,1,0:T(1,128)} %reshape.686), channel_id=1, replica_groups=mesh['px'=16,'py'=8] {'px'}, dimensions={0} | all-to-all | bytes 8388608 | tf_op jit(solution)/shard_map/all_to_all | solution.py:137
  163.6 13.7 %reduce = f32[16,65536]{1,0:T(8,128)} reduce(f32[16,1,65536]{2,1,0:T(1,128)} %all_to_all.72, f32[]{:T(128)} %broadcast.1380), dimensions={1}, to_apply=%all_to_all.52.reduce_sub_computation | reduce | bytes 8388612 | tf_op jit(solution)/shard_map/all_to_all | solution.py:137
  177.3 6.9 %reshape.687 = f32[256,2,32,64]{3,2,1,0:T(8,128)} reshape(f32[16,65536]{1,0:T(8,128)} %reduce) | data formatting | bytes 8388608
  184.3 8.0 %copy.51 = f32[2,16,16,32,64]{4,3,2,1,0:T(8,128)} copy(f32[2,16,16,32,64]{4,3,0,1,2:T(8,128)} %bitcast.530) | data formatting | bytes 8388608 | tf_op jit(solution)/shard_map/all_to_all | solution.py:137
  192.3 6.8 %copy.52 = f32[2,16,512,64]{2,3,0,1:T(8,128)} copy(f32[2,16,512,64]{3,2,1,0:T(8,128)} %bitcast.531) | data formatting | bytes 8388608 | tf_op jit(solution)/shard_map/all_to_all | solution.py:137
  199.1 5.6 all-to-all-start.1
  204.7 3.8 fusion.169
  208.6 3.9 broadcast_multiply_fusion
  212.4 4.3 fusion.167
  216.7 3.2 fusion.139
  219.9 33.5 %all-to-all-done.1 = f32[2,16,512,64]{2,3,0,1:T(8,128)} async-done(((f32[2,16,512,64]{2,3,0,1:T(8,128)}), f32[2,16,512,64]{2,3,0,1:T(8,128)}, u32[]{:S(2)}, u32[]{:S(2)}) %all-to-all-start.1) | async-done | bytes 4194336 | tf_op jit(solution)/shard_map/all_to_all | solution.py:136
  256.3 14.2 %fusion.119 = f32[2,512,2,512,1]{3,1,2,4,0:T(8,128)S(1)} fusion(f32[2,2,512,512,1]{2,3,1,0,4:T(8,128)S(1)} %bitcast.535, f32[1,2,512,512]{2,3,1,0:T(8,128)S(1)} %get-tuple-element.285, f32[1,2,512,512]{2,3,1,0:T(8,128)S(1)} %copy-done.1), kind=kOutput, calls=%fused_computation.141 | convolution fusion | flops 12885950464 | bytes 12582912 | tf_op jit(solution)/shard_map/czxy,dcyk->dzxk/dot_general | solution.py:143
  270.5 14.4 %fusion.116 = f32[2,2,512,512,1]{3,2,1,0,4:T(8,128)S(1)} fusion(f32[2,512,2,512,1]{3,1,2,4,0:T(8,128)S(1)} %fusion.119, f32[1,2,512,512]{2,3,1,0:T(8,128)S(1)} %get-tuple-element.285, f32[1,2,512,512]{2,3,1,0:T(8,128)S(1)} %copy-done.1, f32[2,512,512]{2,1,0:T(8,128)S(1)} %copy-done), kind=kOutput, calls=%fused_computation.138 | convolution fusion | flops 12886999040 | bytes 14680064 | tf_op jit(solution)/shard_map/czxy,dcxk->dzky/dot_general | solution.py:144
  285.0 14.1 %fusion.125 = f32[2,512,2,512,1]{3,1,4,0,2:T(8,128)S(1)} fusion(f32[2,2,512,512,1]{3,2,1,0,4:T(8,128)S(1)} %fusion.116, f32[1,2,512,512]{2,3,1,0:T(8,128)S(1)} %copy-done.5, f32[1,2,512,512]{2,3,1,0:T(8,128)S(1)} %copy-done.4), kind=kOutput, calls=%fused_computation.149 | convolution fusion | flops 12885950464 | bytes 12582912 | tf_op jit(solution)/shard_map/czxy,dcyk->dzxk/dot_general | solution.py:146
  299.1 14.8 %fusion.128 = f32[2,2,512,512]{3,2,1,0:T(8,128)} fusion(f32[2,512,2,512,1]{3,1,4,0,2:T(8,128)S(1)} %fusion.125, f32[1,2,512,512]{2,3,1,0:T(8,128)S(1)} %copy-done.5, f32[1,2,512,512]{2,3,1,0:T(8,128)S(1)} %copy-done.4), kind=kOutput, calls=%fused_computation.160 | convolution fusion | flops 12885950464 | bytes 12582912 | tf_op jit(solution)/shard_map/czxy,dcxk->dzky/dot_general | solution.py:147
  314.0 7.3 %copy.59 = f32[2,2,512,512]{2,1,0,3:T(2,128)} copy(f32[2,2,512,512]{3,2,1,0:T(8,128)} %fusion.128) | data formatting | bytes 8388608 | tf_op jit(solution)/shard_map/czxy,dcxk->dzky/transpose | solution.py:147
  321.3 64.1 %all_to_all.73 = f32[2,2,512,512]{2,1,0,3:T(2,128)S(1)} all-to-all(f32[2,2,512,512]{2,1,0,3:T(2,128)} %copy.59), channel_id=1, replica_groups=mesh['px'=16,'py'=8] {'py'}, dimensions={3} | all-to-all | bytes 8388608 | tf_op jit(solution)/shard_map/all_to_all | solution.py:148
  389.2 9.2 %copy.62 = f32[2,16,512,64]{3,1,0,2:T(8,128)} copy(f32[2,16,512,64]{2,3,1,0:T(8,128)} %bitcast.533) | data formatting | bytes 8388608 | tf_op jit(solution)/shard_map/all_to_all | solution.py:148
  398.4 13.3 %reshape.688 = f32[16,1,65536]{2,1,0:T(1,128)} reshape(f32[512,2,16,64]{3,2,1,0:T(8,128)} %bitcast.528) | data formatting | bytes 8388608
  411.7 58.1 %all_to_all.74 = f32[16,1,65536]{2,1,0:T(1,128)} all-to-all(f32[16,1,65536]{2,1,0:T(1,128)} %reshape.688), channel_id=1, replica_groups=mesh['px'=16,'py'=8] {'px'}, dimensions={0} | all-to-all | bytes 8388608 | tf_op jit(solution)/shard_map/all_to_all | solution.py:149
  469.8 13.7 %reduce.1 = f32[16,65536]{1,0:T(8,128)} reduce(f32[16,1,65536]{2,1,0:T(1,128)} %all_to_all.74, f32[]{:T(128)} %broadcast.1380), dimensions={1}, to_apply=%all_to_all.64.reduce_sub_computation | reduce | bytes 8388612 | tf_op jit(solution)/shard_map/all_to_all | solution.py:149
  483.5 7.3 %reshape.689 = f32[512,2,16,64]{3,2,1,0:T(8,128)} reshape(f32[16,65536]{1,0:T(8,128)} %reduce.1) | data formatting | bytes 8388608
  490.9 8.3 %copy.64 = f32[2,16,16,32,64]{4,3,2,1,0:T(8,128)S(1)} copy(f32[2,16,16,32,64]{4,2,0,3,1:T(8,128)} %bitcast.532) | data formatting | bytes 8388608 | tf_op jit(solution)/shard_map/all_to_all | solution.py:149
  499.2 16.7 %bitcast_multiply_fusion.2 = f32[32,64,256]{2,1,0:T(8,128)S(1)} fusion(f32[2,256,32,64]{3,2,1,0:T(8,128)S(1)} %bitcast.529, f32[1,256,256]{2,1,0:T(8,128)S(1)} %get-tuple-element.302, f32[1,256,256]{2,1,0:T(8,128)S(1)} %copy-done.3), kind=kOutput, calls=%fused_computation.171 | convolution fusion | flops 3221880832 | bytes 6815744 | tf_op jit(solution)/shard_map/ckxy,ckz->xyz/dot_general | solution.py:150
  516.0 5.3 collective-permute-start.5
  535.0 61.5 %while.27 = (s32[]{:T(128)}, f32[8,16,128]{2,1,0:T(8,128)S(1)}, s32[8]{0:T(128)S(1)}, f32[36,68,256]{2,0,1:T(8,128)}, s32[8,16,128]{2,1,0:T(8,128)S(1)}, /*index...) while((s32[]{:T(128)}, f32[8,16,128]{2,1,0:T(8,128)S(1)}, ...), condition=%wide.region_4.5_spmd.clone, body=%wide.region_2.4_spmd.sunk.clone | while | flops 418510848 | bytes 6922475 | solution.py:167
  539.2 3.7 fusion.265
  546.9 3.7 fusion.265
  554.5 3.7 fusion.265
  562.2 3.7 fusion.265
  569.9 3.7 fusion.265
  577.5 3.7 fusion.265
  585.2 3.7 fusion.265
  592.9 3.7 fusion.265
  (210 shorter events, 79.9 us)
Async XLA Ops:
  54.8 4.6 copy-start.6
  60.5 8.5 %collective-permute-start = (f32[2,68,256]{2,1,0:T(8,128)S(1)}, f32[2,68,256]{2,1,0:T(8,128)S(1)}, u32[]{:S(2)}, u32[]{:S(2)}) collective-permute-start(f32[2,68,256]{2,1,0:T(8,128)S(1)} %get-tuple-element.276), channel_id=1, source_target_pairs={{0,8},{8,16},{16,24},{24,32},{32,40},{40,48},{48,56},{56,64},{64,7... | collective-permute-start | bytes 417800 | tf_op jit(solution)/shard_map/ppermute | solution.py:21
  60.6 8.4 %collective-permute-start.1 = (f32[2,68,256]{2,1,0:T(8,128)S(1)}, f32[2,68,256]{2,1,0:T(8,128)S(1)}, u32[]{:S(2)}, u32[]{:S(2)}) collective-permute-start(f32[2,68,256]{2,1,0:T(8,128)S(1)} %get-tuple-element.277), channel_id=1, source_target_pairs={{8,0},{16,8},{24,16},{32,24},{40,32},{48,40},{56,48},{64,56},{72,6... | collective-permute-start | bytes 417800 | tf_op jit(solution)/shard_map/ppermute | solution.py:24
  69.1 6.7 %collective-permute-start.2 = (f32[40,2,256]{2,1,0:T(2,128)S(1)}, f32[40,2,256]{2,1,0:T(2,128)S(1)}, u32[]{:S(2)}, u32[]{:S(2)}) collective-permute-start(f32[40,2,256]{2,1,0:T(2,128)S(1)} %get-tuple-element.274), channel_id=1, source_target_pairs={{0,1},{1,2},{2,3},{3,4},{4,5},{5,6},{6,7},{7,0},{8,9},{9,10},{10,1... | collective-permute-start | bytes 245768 | tf_op jit(solution)/shard_map/ppermute | solution.py:21
  70.7 5.1 collective-permute-start.3
  74.7 2.1 copy-start.2
  199.1 54.4 %all-to-all-start.1 = ((f32[2,16,512,64]{2,3,0,1:T(8,128)}), f32[2,16,512,64]{2,3,0,1:T(8,128)}, u32[]{:S(2)}, u32[]{:S(2)}) async-start(f32[2,16,512,64]{2,3,0,1:T(8,128)} %copy.52), calls=%async_computation.1 | async-start | bytes 8388608 | tf_op jit(solution)/shard_map/all_to_all | solution.py:136
  253.5 2.9 copy-start.1
  256.3 14.2 %copy-start = (f32[2,512,512]{2,1,0:T(8,128)S(1)}, f32[2,512,512]{2,1,0:T(8,128)}, u32[]{:S(2)}) copy-start(f32[2,512,512]{2,1,0:T(8,128)} %param.13) | copy-start | bytes 6291460
  270.5 14.5 %copy-start.4 = (f32[1,2,512,512]{2,3,1,0:T(8,128)S(1)}, f32[1,2,512,512]{2,3,1,0:T(8,128)}, u32[]{:S(2)}) copy-start(f32[1,2,512,512]{2,3,1,0:T(8,128)} %get-tuple-element.284) | copy-start | bytes 6291460
  270.5 14.5 %copy-start.5 = (f32[1,2,512,512]{2,3,1,0:T(8,128)S(1)}, f32[1,2,512,512]{2,3,1,0:T(8,128)}, u32[]{:S(2)}) copy-start(f32[1,2,512,512]{2,3,1,0:T(8,128)} %get-tuple-element.287) | copy-start | bytes 6291460
  490.9 8.3 %copy-start.3 = (f32[1,256,256]{2,1,0:T(8,128)S(1)}, f32[1,256,256]{2,1,0:T(8,128)}, u32[]{:S(2)}) copy-start(f32[1,256,256]{2,1,0:T(8,128)} %copy-done.2) | copy-start | bytes 786436
  515.9 8.1 %collective-permute-start.4 = (f32[2,64,256]{2,1,0:T(8,128)S(1)}, f32[2,64,256]{2,1,0:T(8,128)S(1)}, u32[]{:S(2)}, u32[]{:S(2)}) collective-permute-start(f32[2,64,256]{2,1,0:T(8,128)S(1)} %get-tuple-element.282), channel_id=1, source_target_pairs={{0,8},{8,16},{16,24},{24,32},{32,40},{40,48},{48,56},{56,64},{64,7... | collective-permute-start | bytes 393224 | tf_op jit(solution)/shard_map/ppermute | solution.py:21
  516.0 8.0 %collective-permute-start.5 = (f32[2,64,256]{2,1,0:T(8,128)S(1)}, f32[2,64,256]{2,1,0:T(8,128)S(1)}, u32[]{:S(2)}, u32[]{:S(2)}) collective-permute-start(f32[2,64,256]{2,1,0:T(8,128)S(1)} %get-tuple-element.283), channel_id=1, source_target_pairs={{8,0},{16,8},{24,16},{32,24},{40,32},{48,40},{56,48},{64,56},{72,6... | collective-permute-start | bytes 393224 | tf_op jit(solution)/shard_map/ppermute | solution.py:24
  524.7 6.8 %collective-permute-start.6 = (f32[36,2,256]{2,1,0:T(2,128)}, f32[36,2,256]{2,1,0:T(2,128)}, u32[]{:S(2)}, u32[]{:S(2)}) collective-permute-start(f32[36,2,256]{2,1,0:T(2,128)} %get-tuple-element.278), channel_id=1, source_target_pairs={{0,1},{1,2},{2,3},{3,4},{4,5},{5,6},{6,7},{7,0},{8,9},{9,10},{10,1... | collective-permute-start | bytes 221192 | tf_op jit(solution)/shard_map/ppermute | solution.py:21
  525.9 5.5 collective-permute-start.7
  532.7 2.3 copy-start.7
  535.0 61.5 %copy-start.8 = (s32[8,16]{1,0:T(8,128)S(1)}, s32[8,16]{1,0:T(8,128)}, u32[]{:S(2)}) copy-start(s32[8,16]{1,0:T(8,128)} %param.12) | copy-start | bytes 1540
where the time goes:
time: 607 us; the launch traced here: 598 us
  blocking collectives  180 us (30%)
  matrix products  143 us (24%)
  local copies, waits for them, and re-layouts  142 us (23%)
  other arithmetic  57.1 us (9%)
  waiting for transfers between devices  42.7 us (7%)
  starting transfers between devices  25.5 us (4%)
  loops' own time  6.42 us (1%)
    all_to_all x1, blocking collectives, per_device(): lax.all_to_all(back_x, 'py', split_axis=3, concat_axis=1, tiled=True)  64.1 us
    all_to_all x1, blocking collectives, per_device(): lax.all_to_all(spectrum_z, 'px', split_axis=1, concat_axis=2, tiled=True)  58.3 us
    all_to_all x1, blocking collectives, per_device(): lax.all_to_all(half_back, 'px', split_axis=2, concat_axis=1, tiled=True)  58.1 us
    unnamed x22, local copies, waits for them, and re-layouts  40.9 us
    dot_general x8, matrix products, spread_row(): jnp.einsum('buvs,bzs->buvz', lifted, depth_table_row, precision=exact_prec)  34 us
    all_to_all x1, waiting for transfers between devices, per_device(): lax.all_to_all(lax.all_to_all(spectrum_z, 'px', split_axis=1, concat_axis...  33.5 us
    dot_general x8, matrix products, gather_row(): jnp.einsum('ubvz,bzs->buvs', window, depth_table_row, precision=exact_prec)  29.4 us
    ppermute x4, starting transfers between devices, with_halo(): lax.ppermute(lax.slice_in_dim(block, 0, width, axis=dim), axis, backward)  16.8 us
  transfers between devices with their start and end apart: 9, of which 5 were waited for; matrix products, arithmetic and copies ran while one was open for 3% of the time, Pallas kernels for 0%

commit v1 on v0

v1 whole, which is shorter than its diff:
```python
import jax
import jax.numpy as jnp
import ml_dtypes
import numpy as np
from jax import lax
from jax.experimental import pallas as pl
from jax.experimental.pallas import tpu as pltpu
from jax.sharding import PartitionSpec as P

NX, NY, NZ = 512, 512, 256
PX, PY = 16, 8
DEVICES = PX * PY
MIDDLE = DEVICES // 2
CELLS = 128
ROWS = 40
EXT_X, EXT_Y = 40, 72
BF, F32 = jnp.bfloat16, jnp.float32


def split_np(table):
    high = table.astype(ml_dtypes.bfloat16)
    low = (table - high.astype(np.float64)).astype(ml_dtypes.bfloat16)
    return high, low


def depth_angles():
    device = np.arange(DEVICES)
    wave = np.where(device < MIDDLE, 2 * device + 1, 2 * device)
    return 2.0 * np.pi * ((wave[:, None] * np.arange(NZ)[None, :]) % NZ) / NZ


def depth_tables():
    angle = depth_angles()
    first, second = np.cos(angle), -np.sin(angle)
    second[MIDDLE] = 1.0
    forward = np.concatenate([first, second])
    gain = np.full((DEVICES, 1), 2.0)
    gain[MIDDLE] = 1.0
    inverse = forward * np.concatenate([gain, gain]) / (NX * NY * NZ)
    return np.concatenate(split_np(forward)), np.concatenate(split_np(inverse))


def y_tables():
    tables = []
    for parity in (0, 1):
        wave = 2 * np.arange(256) + parity
        main = 64 * np.arange(4)[:, None] + np.arange(64)[None, :]
        rim = (64 * (np.arange(8)[:, None] + 1) + np.arange(4)[None, :]) % NY

        def pair(position):
            angle = 2.0 * np.pi * ((position[..., None] * wave) % NY) / NY
            cosine, sine = np.cos(angle), np.sin(angle)
            first = np.concatenate([cosine, -sine], axis=-1)
            second = np.concatenate([sine, cosine], axis=-1)
            return first, second

        first, second = pair(main)
        whole = np.stack([first, second], axis=1).reshape(512, 512)
        first, second = pair(rim)
        edge = np.stack([first, second], axis=0).reshape(64, 512)
        whole = np.concatenate([whole, edge, np.zeros((64, 512))])
        tables.append(np.stack(split_np(whole)))
    return np.stack(tables)


def x_tables():
    forward, inverse = [], []
    for parity in (0, 1):
        wave = 2 * np.arange(256) + parity
        angle = 2.0 * np.pi * ((wave[:, None] * np.arange(256)[None, :]) % NX) / NX
        cosine, sine = np.cos(angle), np.sin(angle)
        forward.append(np.concatenate(split_np(np.concatenate([cosine, sine]))))
        inverse.append(np.concatenate(split_np(np.concatenate([cosine.T, sine.T]))))
    return np.stack(forward + inverse)


def turn_tables():
    index = np.arange(256)
    even = np.zeros((256, 256))
    even[index, (256 - index) % 256] = 1.0
    odd = np.zeros((256, 256))
    odd[index, 255 - index] = 1.0
    return np.stack([even, odd]).astype(ml_dtypes.bfloat16)


def sort_table():
    index = np.arange(512)
    order = np.zeros((512, 512))
    order[index, (index % 2) * 256 + index // 2] = 1.0
    return order.astype(ml_dtypes.bfloat16)


def split(value):
    high = value.astype(BF)
    low = (value - high.astype(F32)).astype(BF)
    return high, low


def dot(left, right):
    return lax.dot_general(left, right, (((1,), (0,)), ((), ())), preferred_element_type=F32)


def dot_nt(left, right):
    return lax.dot_general(left, right, (((1,), (1,)), ((), ())), preferred_element_type=F32)


def spline_weights(fractions):
    values = [fractions, 1.0 - fractions]
    for degree in (3, 4, 5):
        updated = []
        for position in range(degree):
            term = None
            if position < degree - 1:
                term = (fractions + float(position)) * values[position]
            if position >= 1:
                lower = (float(degree - position) - fractions) * values[position - 1]
                term = lower if term is None else term + lower
            updated.append(term * (1.0 / (degree - 1)))
        values = updated
    return values


def pick(selected, weights):
    total = jnp.where(selected == 4, weights[4], 0.0)
    for degree in (3, 2, 1, 0):
        total = jnp.where(selected == degree, weights[degree], total)
    return total


def occupied_rows(count_ref, chunk):
    sub = lax.broadcasted_iota(jnp.int32, (8, 128), 0)
    slot = lax.broadcasted_iota(jnp.int32, (8, 128), 1)
    counts = jnp.zeros((8, 128), jnp.int32)
    for row in range(8):
        counts = jnp.where(sub == row, count_ref[chunk // 2, (chunk % 2) * 8 + row], counts)
    return slot < counts


def prepare(frac_ref, base_ref, wx_ref, wy_ref, wz_ref, charge_of):
    def chunk_step(chunk, carry):
        rows = pl.ds(pl.multiple_of(chunk * 8, 8), 8)
        weights = spline_weights(frac_ref[0, rows, :])
        offset = (base_ref[0, rows, :] & 3) + 4
        charge = charge_of(chunk, rows)
        for position in range(8):
            window = pick(offset - position, weights)
            wx_ref[position, rows, :] = window if charge is None else window * charge
        for degree, weight in enumerate(spline_weights(frac_ref[1, rows, :])):
            wy_ref[degree, rows, :] = weight
        for degree, weight in enumerate(spline_weights(frac_ref[2, rows, :])):
            wz_ref[degree, rows, :] = weight
        return carry

    lax.fori_loop(0, CELLS // 8, chunk_step, 0)


def depth_weights(base_ref, wz_ref, cell):
    row = pl.ds(cell, 1)
    level = lax.broadcasted_iota(jnp.int32, (NZ, 128), 0)
    selected = ((base_ref[2, row, :] + 2) - level) & (NZ - 1)
    return split(pick(selected, [wz_ref[degree, row, :] for degree in range(5)]))


def pair_depth(base_ref, wz_ref, cell):
    first = depth_weights(base_ref, wz_ref, cell)
    second = depth_weights(base_ref, wz_ref, cell + 1)
    return (
        jnp.concatenate([first[0], second[0]], axis=1),
        jnp.concatenate([first[1], second[1]], axis=1),
    )


def pair_window_y(base_ref, wy_ref, cell):
    parts = []
    for side in (0, 1):
        row = pl.ds(cell + side, 1)
        position = lax.broadcasted_iota(jnp.int32, (16, 128), 0)
        selected = ((base_ref[1, row, :] & 3) + 4 + 4 * side) - position
        parts.append(pick(selected, [wy_ref[degree, row, :] for degree in range(5)]))
    return jnp.concatenate(parts, axis=1)


def pair_row(ref, position, cell):
    return jnp.concatenate(
        [ref[position, pl.ds(cell, 1), :], ref[position, pl.ds(cell + 1, 1), :]], axis=1
    )


def spread_kernel(
    count_ref, cot_ref, frac_ref, base_ref, table_ref, out_ref, ext_ref, wx_ref, wy_ref, wz_ref
):
    def charge_of(chunk, rows):
        return jnp.where(occupied_rows(count_ref, chunk), cot_ref[rows, :], 0.0)

    prepare(frac_ref, base_ref, wx_ref, wy_ref, wz_ref, charge_of)

    def clear(step, carry):
        rows = pl.ds(pl.multiple_of(step * EXT_Y, 8), EXT_Y)
        for half in (0, 1):
            ext_ref[half, rows, :] = jnp.zeros((EXT_Y, 128), F32)
        return carry

    lax.fori_loop(0, EXT_X, clear, 0)

    def pair_step(step, carry):
        cell_x, pair = step // 8, step % 8
        cell = step * 2
        depth_high, depth_low = pair_depth(base_ref, wz_ref, cell)
        window_y = pair_window_y(base_ref, wy_ref, cell)
        lifted = jnp.concatenate(
            [pair_row(wx_ref, u, cell) * window_y for u in range(8)], axis=0
        )
        high, low = split(lifted)
        both = dot_nt(jnp.concatenate([high, low], axis=0), depth_high)
        patch = both[:128] + both[128:] + dot_nt(high, depth_low)
        for u in range(8):
            rows = pl.ds(pl.multiple_of((cell_x * 4 + u) * EXT_Y + pair * 8, 8), 16)
            for half in (0, 1):
                ext_ref[half, rows, :] += patch[16 * u : 16 * u + 16, 128 * half : 128 * half + 128]
        return carry

    lax.fori_loop(0, CELLS // 2, pair_step, 0)

    lane = lax.broadcasted_iota(jnp.int32, (128, 128), 1)

    def transform(blocks, first_row):
        high, low = split(jnp.concatenate(blocks, axis=0))
        both = dot_nt(table_ref[...], high)
        planes = both[:256] + both[256:] + dot_nt(table_ref[:256], low)
        for duo in (0, 1):
            first = planes[:128, 128 * duo : 128 * duo + 128]
            second = planes[128:, 128 * duo : 128 * duo + 128]
            left = jnp.where(lane < 64, first, pltpu.roll(second, 64, 1))
            right = jnp.where(lane < 64, pltpu.roll(first, 64, 1), second)
            out_ref[pl.ds(first_row + 2 * duo, 128, stride=ROWS), :] = left
            out_ref[pl.ds(first_row + 2 * duo + 1, 128, stride=ROWS), :] = right

    def row_step(step, carry):
        blocks = []
        for row in range(4):
            rows = pl.ds(pl.multiple_of((step * 4 + row) * EXT_Y, 8), 64)
            blocks.append(jnp.concatenate([ext_ref[0, rows, :], ext_ref[1, rows, :]], axis=1))
        transform(blocks, step * 4)
        return carry

    lax.fori_loop(0, 9, row_step, 0)
    blocks = []
    for rim in range(4):
        rows = pl.ds(64 + rim, EXT_X, stride=EXT_Y)
        block = jnp.concatenate([ext_ref.at[0][rows, :], ext_ref.at[1][rows, :]], axis=1)
        blocks.append(jnp.concatenate([block, jnp.zeros((24, 256), F32)], axis=0))
    transform(blocks, 36)


def plane_kernel(
    flag_ref,
    in_ref,
    influence_hbm,
    zero_hbm,
    y_hbm,
    x_hbm,
    turn_hbm,
    sort_hbm,
    out_ref,
    influence,
    zero_plane,
    y_table,
    x_table,
    turn,
    sort,
    block_high,
    block_low,
    sorted_influence,
    sorted_difference,
    spectrum,
    result,
    sems,
):
    plane, middle = flag_ref[0], flag_ref[1]
    moves = [(sort_hbm, sort), (y_hbm, y_table), (x_hbm, x_table), (turn_hbm, turn)]
    for part in range(4):
        columns = pl.ds(128 * part, 128)
        moves.append((influence_hbm.at[plane, :, columns], influence.at[part]))
        moves.append((zero_hbm.at[:, columns], zero_plane.at[part]))
    copies = [
        pltpu.make_async_copy(source, target, sems.at[index])
        for index, (source, target) in enumerate(moves)
    ]
    for copy in copies:
        copy.start()

    sub = lax.broadcasted_iota(jnp.int32, (8, 128), 0)
    lane = lax.broadcasted_iota(jnp.int32, (32, 128), 1)
    lane8 = lax.broadcasted_iota(jnp.int32, (8, 128), 1)

    def block_rows(p, q, first, count):
        return pl.ds(pl.multiple_of((p * PY + q) * ROWS + first, 8), count)

    def rim_rows(p):
        tiles = []
        for q in range(0, PY, 2):
            even = in_ref[block_rows(p, q, 32, 8), :]
            odd = in_ref[block_rows(p, q + 1, 32, 8), :]
            tiles.append(jnp.where(sub < 4, pltpu.roll(even, 4, 0), odd))
        tiles.append(jnp.zeros((96, 128), F32))
        return jnp.concatenate(tiles, axis=0).T

    def main_rows(p, q):
        own = in_ref[block_rows(p, q, 0, 32), :]
        edge = in_ref[block_rows((p + PX - 1) % PX, q, 32, 8), :]
        return jnp.concatenate([own[:8] + jnp.where(sub < 4, edge, 0.0), own[8:]], axis=0)

    def edge_rows(p):
        turned, before = rim_rows(p), rim_rows((p + PX - 1) % PX)
        own = turned[0:32] + pltpu.roll(turned[64:96], 32, 1)
        edge = before[32:40] + pltpu.roll(before[96:104], 32, 1)
        first = own[:8] + jnp.where(sub < 4, edge, 0.0)
        return jnp.concatenate([first, own[8:]], axis=0)

    def assemble(p, carry):
        rows = pl.ds(pl.multiple_of(p * 32, 32), 32)

        def put(parity, columns, value):
            high, low = split(value)
            block_high[parity, rows, columns] = high
            block_low[parity, rows, columns] = low

        for q in range(4):
            columns = pl.ds(128 * q, 128)
            a, b = main_rows(p, q), main_rows(p, q + 4)
            c, d = main_rows(p + 8, q), main_rows(p + 8, q + 4)
            even, odd = a + b, a - b
            even_far, odd_far = c + d, c - d
            put(0, columns, even + even_far)
            put(1, columns, odd + odd_far)
            put(2, columns, even - even_far)
            put(3, columns, odd - odd_far)
        near, far = edge_rows(p), edge_rows(p + 8)
        columns = pl.ds(512, 128)
        for parity in (0, 1):
            put(parity, columns, near + far)
            put(parity + 2, columns, near - far)
        return carry

    lax.fori_loop(0, 8, assemble, 0)

    def sorted_columns(value):
        high, low = split(value)
        return dot(high, sort[...]) + dot(low, sort[...])

    for copy in copies:
        copy.wait()

    half = middle.astype(F32) * 0.5
    for f in (0, 1):
        rows = pl.ds(f, 256, stride=2)
        own = jnp.concatenate([influence.at[part][rows, :] for part in range(4)], axis=1)
        for_sorting = own

        @pl.when(middle == 0)
        def _plain():
            value = sorted_columns(for_sorting)
            for e in (0, 1):
                sorted_influence[2 * f + e] = value[:, 256 * e : 256 * e + 256]

        @pl.when(middle != 0)
        def _mixed():
            other = jnp.concatenate([zero_plane.at[part][rows, :] for part in range(4)], axis=1)
            total = sorted_columns((for_sorting + other) * half)
            difference = sorted_columns((for_sorting - other) * half)
            for e in (0, 1):
                sorted_influence[2 * f + e] = total[:, 256 * e : 256 * e + 256]
                sorted_difference[2 * f + e] = difference[:, 256 * e : 256 * e + 256]

    def left_products(table, value):
        high, low = split(value)
        both = dot(table, high)
        total = both[:512] + both[512:] + dot(table[:512], low)
        return total[:256], total[256:]

    for f in (0, 1):
        for e in (0, 1):
            which = 2 * f + e
            high, low = block_high[which], block_low[which]
            table_high, table_low = y_table[e, 0], y_table[e, 1]
            both = dot(jnp.concatenate([high, low], axis=0), table_high)
            along_y = both[:256] + both[256:] + dot(high, table_low)
            forward = x_table[f]
            cos_re, sin_re = left_products(forward, along_y[:, :256])
            cos_im, sin_im = left_products(forward, along_y[:, 256:])
            real, imag = cos_re + sin_im, cos_im - sin_re
            weight = sorted_influence[which]
            spectrum[0] = real * weight
            spectrum[1] = imag * weight

            @pl.when(middle != 0)
            def _add_turned():
                def turned(value):
                    high, low = split(value)
                    part = dot(turn[f], high) + dot(turn[f], low)
                    high, low = split(part)
                    return dot(high, turn[e]) + dot(low, turn[e])

                weight = sorted_difference[which]
                spectrum[0] += turned(real) * weight
                spectrum[1] -= turned(imag) * weight

            inverse = x_table[2 + f]
            cos_re, sin_re = left_products(inverse, spectrum[0])
            cos_im, sin_im = left_products(inverse, spectrum[1])
            back = jnp.concatenate([cos_re - sin_im, cos_im + sin_re], axis=1)
            high, low = split(back)
            both = dot_nt(jnp.concatenate([high, low], axis=0), table_high)
            result[which] = both[:256] + both[256:] + dot_nt(high, table_low)

    def four(rows, columns):
        a, b = result[0, rows, columns], result[1, rows, columns]
        c, d = result[2, rows, columns], result[3, rows, columns]
        return a, b, c, d

    def send(p, carry):
        rows = pl.ds(pl.multiple_of(p * 32, 32), 32)
        after = pl.ds(pl.multiple_of(((p + 1) % 8) * 32, 32), 8)
        wrap = jnp.where(p == 7, -1.0, 1.0)
        columns = pl.ds(512, 128)
        a, b, c, d = four(rows, columns)
        a1, b1, c1, d1 = four(after, columns)
        rims = []
        for sign in (1.0, -1.0):
            own = (a + b) + sign * (c + d)
            edge = (a1 + b1) + (sign * wrap) * (c1 + d1)
            tall = jnp.concatenate([own, edge, jnp.zeros((88, 128), F32)], axis=0).T
            rims.append(tall[0:32] + pltpu.roll(tall[32:64], 64, 1))
        for q in range(4):
            columns = pl.ds(128 * q, 128)
            a, b, c, d = four(rows, columns)
            a1, b1, c1, d1 = four(after, columns)
            for side, y_sign in ((0, 1.0), (4, -1.0)):
                even, odd = a + y_sign * b, c + y_sign * d
                even1, odd1 = a1 + y_sign * b1, c1 + y_sign * d1
                for far, x_sign in ((0, 1.0), (8, -1.0)):
                    target_q, target_p = q + side, p + far
                    out_ref[block_rows(target_p, target_q, 0, 32), :] = even + x_sign * odd
                    edge = even1 + (x_sign * wrap) * odd1
                    tile = rims[far // 8][8 * (target_q // 2) : 8 * (target_q // 2) + 8]
                    if target_q % 2 == 0:
                        tile = pltpu.roll(tile, 4, 0)
                    out_ref[block_rows(target_p, target_q, 32, 8), :] = jnp.where(
                        sub < 4, edge, tile
                    )
        return carry

    lax.fori_loop(0, 8, send, 0)


def gather_kernel(
    count_ref, in_ref, frac_ref, base_ref, table_ref, out_ref, ext_ref, wx_ref, wy_ref, wz_ref
):
    prepare(frac_ref, base_ref, wx_ref, wy_ref, wz_ref, lambda chunk, rows: None)

    def inverse(first_row):
        blocks = []
        for row in range(4):
            block = in_ref[pl.ds(first_row + row, 128, stride=ROWS), :].T
            blocks.append(jnp.concatenate([block[:64], block[64:]], axis=1))
        high, low = split(jnp.concatenate(blocks, axis=0))
        both = dot(jnp.concatenate([high, low], axis=0), table_ref[:256])
        return both[:256] + both[256:] + dot(high, table_ref[256:])

    def row_step(step, carry):
        values = inverse(step * 4)
        for row in range(4):
            start = (step * 4 + row) * EXT_Y
            rows = pl.ds(pl.multiple_of(start, 8), 64)
            last = pl.ds(pl.multiple_of(start + 64, 8), 8)
            for half in (0, 1):
                ext_ref[half, rows, :] = values[64 * row : 64 * row + 64, 128 * half : 128 * half + 128]
                ext_ref[half, last, :] = jnp.zeros((8, 128), F32)
        return carry

    lax.fori_loop(0, 9, row_step, 0)
    values = inverse(36)
    for rim in range(4):
        rows = pl.ds(64 + rim, EXT_X, stride=EXT_Y)
        for half in (0, 1):
            ext_ref.at[half][rows, :] = values[64 * rim : 64 * rim + EXT_X, 128 * half : 128 * half + 128]

    def pair_step(step, carry):
        cell_x, pair = step // 8, step % 8
        cell = step * 2
        depth_high, depth_low = pair_depth(base_ref, wz_ref, cell)
        windows = []
        for u in range(8):
            rows = pl.ds(pl.multiple_of((cell_x * 4 + u) * EXT_Y + pair * 8, 8), 16)
            windows.append(jnp.concatenate([ext_ref[0, rows, :], ext_ref[1, rows, :]], axis=1))
        high, low = split(jnp.concatenate(windows, axis=0))
        both = dot(jnp.concatenate([high, low], axis=0), depth_high)
        part = both[:128] + both[128:] + dot(high, depth_low)
        total = part[:16] * pair_row(wx_ref, 0, cell)
        for u in range(1, 8):
            total += part[16 * u : 16 * u + 16] * pair_row(wx_ref, u, cell)
        total = jnp.sum(total * pair_window_y(base_ref, wy_ref, cell), axis=0, keepdims=True)
        out_ref[pl.ds(cell, 1), :] = total[:, :128]
        out_ref[pl.ds(cell + 1, 1), :] = total[:, 128:]
        return carry

    lax.fori_loop(0, CELLS // 2, pair_step, 0)

    def mask_step(chunk, carry):
        rows = pl.ds(pl.multiple_of(chunk * 8, 8), 8)
        out_ref[rows, :] = jnp.where(occupied_rows(count_ref, chunk), out_ref[rows, :], 0.0)
        return carry

    lax.fori_loop(0, CELLS // 8, mask_step, 0)


VMEM = pl.BlockSpec(memory_space=pltpu.VMEM)
SMEM = pl.BlockSpec(memory_space=pltpu.SMEM)
ANY = pl.BlockSpec(memory_space=pl.ANY)
PARAMS = pltpu.CompilerParams(vmem_limit_bytes=56 * 1024 * 1024)


def cell_scratch():
    return [
        pltpu.VMEM((2, EXT_X * EXT_Y, 128), F32),
        pltpu.VMEM((8, CELLS, 128), F32),
        pltpu.VMEM((5, CELLS, 128), F32),
        pltpu.VMEM((5, CELLS, 128), F32),
    ]


def per_device(cotangent, fraction, grid_base, cell_count, influence):
    device = lax.axis_index("px") * PY + lax.axis_index("py")
    flags = jnp.stack([(device < MIDDLE).astype(jnp.int32), (device == MIDDLE).astype(jnp.int32)])
    zero_plane = lax.ppermute(influence[0], ("px", "py"), [(0, MIDDLE)])
    fraction = fraction.reshape(3, CELLS, 128)
    grid_base = grid_base.reshape(3, CELLS, 128)
    forward_z, inverse_z = depth_tables()

    sent = pl.pallas_call(
        spread_kernel,
        out_shape=jax.ShapeDtypeStruct((DEVICES * ROWS, 128), F32),
        in_specs=[SMEM, VMEM, VMEM, VMEM, VMEM],
        out_specs=VMEM,
        scratch_shapes=cell_scratch(),
        compiler_params=PARAMS,
        cost_estimate=pl.CostEstimate(flops=10**10, bytes_accessed=10**7, transcendentals=0),
        name="spread",
    )(cell_count, cotangent.reshape(CELLS, 128), fraction, grid_base, forward_z)

    def exchange(array):
        array = array.reshape(DEVICES, ROWS, 128)
        array = lax.all_to_all(array, ("px", "py"), split_axis=0, concat_axis=0, tiled=True)
        return array.reshape(DEVICES * ROWS, 128)

    sent, zero_plane = lax.optimization_barrier((sent, zero_plane))
    planes = exchange(sent)
    back = pl.pallas_call(
        plane_kernel,
        out_shape=jax.ShapeDtypeStruct((DEVICES * ROWS, 128), F32),
        in_specs=[SMEM, VMEM, ANY, ANY, ANY, ANY, ANY, ANY],
        out_specs=VMEM,
        scratch_shapes=[
            pltpu.VMEM((4, 512, 128), F32),
            pltpu.VMEM((4, 512, 128), F32),
            pltpu.VMEM((2, 2, 640, 512), BF),
            pltpu.VMEM((4, 1024, 256), BF),
            pltpu.VMEM((2, 256, 256), BF),
            pltpu.VMEM((512, 512), BF),
            pltpu.VMEM((4, 256, 640), BF),
            pltpu.VMEM((4, 256, 640), BF),
            pltpu.VMEM((4, 256, 256), F32),
            pltpu.VMEM((4, 256, 256), F32),
            pltpu.VMEM((2, 256, 256), F32),
            pltpu.VMEM((4, 256, 640), F32),
            pltpu.SemaphoreType.DMA((12,)),
        ],
        compiler_params=PARAMS,
        name="planes",
    )(
        flags,
        planes,
        influence,
        zero_plane,
        y_tables(),
        x_tables(),
        turn_tables(),
        sort_table(),
    )
    returned = exchange(back)

    gradient = pl.pallas_call(
        gather_kernel,
        out_shape=jax.ShapeDtypeStruct((CELLS, 128), F32),
        in_specs=[SMEM, VMEM, VMEM, VMEM, VMEM],
        out_specs=VMEM,
        scratch_shapes=cell_scratch(),
        compiler_params=PARAMS,
        name="gather",
    )(cell_count, returned, fraction, grid_base, inverse_z)
    return gradient.reshape(cotangent.shape)


def solution(mesh):
    placed = (
        P("px", "py", None),
        P(None, "px", "py", None),
        P(None, "px", "py", None),
        P("px", "py"),
        P(("px", "py"), None, None),
    )
    return jax.shard_map(
        per_device, mesh=mesh, in_specs=placed, out_specs=P("px", "py", None), check_vma=False
    )
```

time: 607 us -> 170 us (0.28); the launches traced: 598 us -> 170 us
  matrix products: 143 us -> 0 us
  blocking collectives: 180 us -> 41.2 us
  local copies, waits for them, and re-layouts: 142 us -> 3.81 us
  Pallas kernels: 0 us -> 77.1 us
  other arithmetic: 57.1 us -> 0.66 us
  starting transfers between devices: 25.5 us -> 11.9 us
  waiting for transfers between devices: 42.7 us -> 34.9 us
  loops' own time: 6.42 us -> 0 us
    dot_general x22 -> x0, matrix products: 143 us -> none  [the longest x8 34 us: spread_row(): jnp.einsum('buvs,bzs->buvz', lifted, depth_table_row, precision=exact_prec)]
    all_to_all x3 -> x1, blocking collectives: 180 us -> 41.2 us  [exchange(): lax.all_to_all(array, ('px', 'py'), split_axis=0, concat_axis=0, tiled=True)]
    pallas_call x0 -> x3, Pallas kernels: none -> 77.1 us  [the longest x1 28.5 us: per_device(): pl.pallas_call(spread_kernel, out_shape=jax.ShapeDtypeStruct((DEVICES * R...]
    all_to_all x8 -> x0, local copies, waits for them, and re-layouts: 39.5 us -> none  [the longest x3 15.3 us: per_device(): lax.all_to_all(spectrum_z, 'px', split_axis=1, concat_axis=2, tiled=True)]
    unnamed x22 -> x4, local copies, waits for them, and re-layouts: 40.9 us -> 2.52 us
    all_to_all x2 -> x0, other arithmetic: 27.5 us -> none  [the longest x1 13.7 us: per_device(): lax.all_to_all(half_back, 'px', split_axis=2, concat_axis=1, tiled=True)]
    dynamic_slice x16 -> x0, local copies, waits for them, and re-layouts: 15.4 us -> none  [the longest x8 10.7 us: gather_row(): stripe = lax.dynamic_slice_in_dim(halo_potential, row_index * CELL, 8, 0)]
    ppermute x8 -> x1, starting transfers between devices: 19.9 us -> 5.93 us  [per_device(): zero_plane = lax.ppermute(influence[0], ('px', 'py'), [(0, MIDDLE)])]
  transfers between devices with their start and end apart: 9 -> 2, of which waited for: 5 -> 1; matrix products, arithmetic and copies ran while one was open for 3% -> 0% of each run, Pallas kernels for 0% -> 17%
where the time goes in v1:
time: 170 us
  Pallas kernels  77.1 us (45%)
  blocking collectives  41.2 us (24%)
  waiting for transfers between devices  34.9 us (21%)
  starting transfers between devices  11.9 us (7%)
  local copies, waits for them, and re-layouts  3.81 us (2%)
    all_to_all x1, blocking collectives, exchange(): lax.all_to_all(array, ('px', 'py'), split_axis=0, concat_axis=0, tiled=True)  41.2 us
    all_to_all x1, waiting for transfers between devices, exchange(): lax.all_to_all(array, ('px', 'py'), split_axis=0, concat_axis=0, tiled=True)  34.9 us
    pallas_call x1, Pallas kernels, per_device(): pl.pallas_call(spread_kernel, out_shape=jax.ShapeDtypeStruct((DEVICES * R...  28.5 us
    pallas_call x1, Pallas kernels, per_device(): pl.pallas_call(gather_kernel, out_shape=jax.ShapeDtypeStruct((CELLS, 128)...  27.3 us
    pallas_call x1, Pallas kernels, per_device(): pl.pallas_call(plane_kernel, out_shape=jax.ShapeDtypeStruct((DEVICES * RO...  21.3 us
    all_to_all x1, starting transfers between devices, exchange(): lax.all_to_all(array, ('px', 'py'), split_axis=0, concat_axis=0, tiled=True)  5.94 us
    ppermute x1, starting transfers between devices, per_device(): zero_plane = lax.ppermute(influence[0], ('px', 'py'), [(0, MIDDLE)])  5.93 us
  transfers between devices with their start and end apart: 2, of which 1 were waited for; matrix products, arithmetic and copies ran while one was open for 0% of the time, Pallas kernels for 17%

profile of v1, /device:TPU:0, one launch (start us, length us, event | category | flops | bytes accessed | tf_op | source)
XLA Modules:
  0.0 169.6 jit_solution(12711698506083311703)
XLA Ops:
  0.0 1.3 slice_bitcast_fusion
  1.3 5.9 %collective-permute-start = (f32[512,512]{1,0:T(8,128)S(1)}, f32[512,512]{1,0:T(8,128)S(1)}, u32[]{:S(2)}, u32[]{:S(2)}) collective-permute-start(f32[512,512]{1,0:T(8,128)S(1)} %slice_bitcast_fusion), channel_id=1, source_target_pairs={{0,64}} | collective-permute-start | bytes 3145736 | tf_op jit(solution)/shard_map/ppermute | solution.py:535
  7.2 28.5 %spread.1 = f32[5120,128]{1,0:T(8,128)} custom-call(s32[8,16]{1,0:T(8,128)} %count_ref.3, f32[128,128]{1,0:T(8,128)} %bitcast.20, f32[3,128,128]{2,1,0:T(8,128)} %bitcast.16, s32[3,128,128]{2,1,0:T(8,128)} %bitcast.18, bf16[512,256]{1,0:T(8,128)(2,1)} %constant.25.clone.table_ref), custom_call_target="tpu_custom_call" | custom-call | flops 10000000000 | bytes 10000000 | tf_op jit(solution)/shard_map/spread/pallas_call | solution.py:540
  35.7 0.0 collective-permute-done.zero_hbm
  35.7 0.0 copy-start.1
  35.7 1.0 copy-done.1
  36.7 5.9 %all-to-all-start = ((f32[128,40,128]{2,1,0:T(8,128)}), f32[128,40,128]{2,1,0:T(8,128)S(1)}, u32[]{:S(2)}, u32[]{:S(2)}) async-start(f32[128,40,128]{2,1,0:T(8,128)} %bitcast.15), calls=%async_computation | async-start | bytes 5242880 | tf_op jit(solution)/shard_map/all_to_all | solution.py:553
  42.7 0.7 add_convert_fusion.flag_ref
  43.4 34.9 %all-to-all-done = f32[128,40,128]{2,1,0:T(8,128)S(1)} async-done(((f32[128,40,128]{2,1,0:T(8,128)}), f32[128,40,128]{2,1,0:T(8,128)S(1)}, u32[]{:S(2)}, u32[]{:S(2)}) %all-to-all-start) | async-done | bytes 2621472 | tf_op jit(solution)/shard_map/all_to_all | solution.py:553
  78.3 0.0 copy-start
  78.3 1.5 copy-done
  79.8 21.3 %planes.1 = f32[5120,128]{1,0:T(8,128)} custom-call(s32[2]{0:T(128)} %add_convert_fusion.flag_ref, f32[5120,128]{1,0:T(8,128)} %bitcast.13, f32[2,512,512]{2,1,0:T(8,128)} %influence_hbm.1, f32[512,512]{1,0:T(8,128)} %copy-done.1, bf16[2,2,640,512]{3,2,1,0:T(8,128)(2,1)} %constant.26.clone.y_hbm, bf16[4,1024,256]{2,1,0:T(8,128)(2,1)} %constant.27.clone.x_hbm, ...), custom_call_target="tpu_custom_call" | custom-call | tf_op jit(solution)/shard_map/planes/pallas_call | solution.py:558
  101.1 41.2 %all_to_all.10 = f32[128,40,128]{2,1,0:T(8,128)} all-to-all(f32[128,40,128]{2,1,0:T(8,128)} %bitcast.14), channel_id=1, replica_groups=mesh['px'=16,'py'=8] {'px','py'}, dimensions={0} | all-to-all | bytes 5242880 | tf_op jit(solution)/shard_map/all_to_all | solution.py:553
  142.3 27.3 %gather.1 = f32[128,128]{1,0:T(8,128)} custom-call(s32[8,16]{1,0:T(8,128)} %count_ref.3, f32[5120,128]{1,0:T(8,128)} %bitcast.12, f32[3,128,128]{2,1,0:T(8,128)} %bitcast.17, s32[3,128,128]{2,1,0:T(8,128)} %bitcast.19, bf16[512,256]{1,0:T(8,128)(2,1)} %constant.30.clone.table_ref), custom_call_target="tpu_custom_call" | custom-call | tf_op jit(solution)/shard_map/gather/pallas_call | solution.py:592
Async XLA Ops:
  1.3 34.4 %collective-permute-start = (f32[512,512]{1,0:T(8,128)S(1)}, f32[512,512]{1,0:T(8,128)S(1)}, u32[]{:S(2)}, u32[]{:S(2)}) collective-permute-start(f32[512,512]{1,0:T(8,128)S(1)} %slice_bitcast_fusion), channel_id=1, source_target_pairs={{0,64}} | collective-permute-start | bytes 3145736 | tf_op jit(solution)/shard_map/ppermute | solution.py:535
  35.7 1.0 copy-start.1
  36.7 41.5 %all-to-all-start = ((f32[128,40,128]{2,1,0:T(8,128)}), f32[128,40,128]{2,1,0:T(8,128)S(1)}, u32[]{:S(2)}, u32[]{:S(2)}) async-start(f32[128,40,128]{2,1,0:T(8,128)} %bitcast.15), calls=%async_computation | async-start | bytes 5242880 | tf_op jit(solution)/shard_map/all_to_all | solution.py:553
  78.3 1.5 copy-start

commit v2 on v1

v2 whole, which is shorter than its diff:
```python
import jax
import jax.numpy as jnp
import ml_dtypes
import numpy as np
from jax import lax
from jax.experimental import pallas as pl
from jax.experimental.pallas import tpu as pltpu
from jax.sharding import PartitionSpec as P

NX, NY, NZ = 512, 512, 256
PX, PY = 16, 8
DEVICES = PX * PY
MIDDLE = DEVICES // 2
CELLS = 128
ROWS = 40
EXT_X, EXT_Y = 40, 72
BF, F32 = jnp.bfloat16, jnp.float32


def split_np(table):
    high = table.astype(ml_dtypes.bfloat16)
    low = (table - high.astype(np.float64)).astype(ml_dtypes.bfloat16)
    return high, low


def depth_angles():
    device = np.arange(DEVICES)
    wave = np.where(device < MIDDLE, 2 * device + 1, 2 * device)
    return 2.0 * np.pi * ((wave[:, None] * np.arange(NZ)[None, :]) % NZ) / NZ


def depth_tables():
    angle = depth_angles()
    first, second = np.cos(angle), -np.sin(angle)
    second[MIDDLE] = 1.0
    forward = np.concatenate([first, second])
    gain = np.full((DEVICES, 1), 2.0)
    gain[MIDDLE] = 1.0
    inverse = forward * np.concatenate([gain, gain]) / (NX * NY * NZ)
    return np.concatenate(split_np(forward)), np.concatenate(split_np(inverse))


def y_tables():
    tables = []
    for residue in range(4):
        wave = 4 * np.arange(128) + residue
        main = 64 * np.arange(2)[:, None] + np.arange(64)[None, :]
        rim = (64 * (np.arange(8)[:, None] + 1) + np.arange(4)[None, :]) % NY

        def pair(position):
            angle = 2.0 * np.pi * ((position[..., None] * wave) % NY) / NY
            cosine, sine = np.cos(angle), np.sin(angle)
            first = np.concatenate([cosine, -sine], axis=-1)
            second = np.concatenate([sine, cosine], axis=-1)
            return first, second

        whole = np.stack(pair(main), axis=1).reshape(256, 256)
        edge = np.stack(pair(rim), axis=0).reshape(64, 256)
        whole = np.concatenate([whole, edge, np.zeros((64, 256))])
        tables.extend(split_np(whole))
    return np.concatenate(tables)


def x_tables():
    forward, inverse = [], []
    for parity in (0, 1):
        wave = 2 * np.arange(256) + parity
        angle = 2.0 * np.pi * ((wave[:, None] * np.arange(256)[None, :]) % NX) / NX
        cosine, sine = np.cos(angle), np.sin(angle)
        forward.append(np.concatenate(split_np(np.concatenate([cosine, sine]))))
        inverse.append(np.concatenate(split_np(np.concatenate([cosine.T, sine.T]))))
    return np.concatenate(forward + inverse[1:])


def turn_tables():
    tables = []
    for size in (256, 128):
        index = np.arange(size)
        for shift in (0, 1):
            table = np.zeros((size, size))
            table[index, (size - shift - index) % size] = 1.0
            tables.append(np.kron(np.eye(256 // size), table))
    return np.concatenate(tables).astype(ml_dtypes.bfloat16)


Y_ROWS, X_ROWS, TURN_ROWS = 8 * 384, 3 * 1024, 4 * 256
X_START, TURN_START = Y_ROWS, Y_ROWS + X_ROWS
TABLE_ROWS = Y_ROWS + X_ROWS + TURN_ROWS


def plane_tables():
    return np.concatenate([y_tables(), x_tables(), turn_tables()])


def sort_table():
    index = np.arange(512)
    order = np.zeros((512, 512))
    order[index, (index % 4) * 128 + index // 4] = 1.0
    return order.astype(ml_dtypes.bfloat16)


def split(value):
    high = value.astype(BF)
    low = (value - high.astype(F32)).astype(BF)
    return high, low


def dot(left, right):
    return lax.dot_general(left, right, (((1,), (0,)), ((), ())), preferred_element_type=F32)


def dot_nt(left, right):
    return lax.dot_general(left, right, (((1,), (1,)), ((), ())), preferred_element_type=F32)


def spline_weights(fractions):
    values = [fractions, 1.0 - fractions]
    for degree in (3, 4, 5):
        updated = []
        for position in range(degree):
            term = None
            if position < degree - 1:
                term = (fractions + float(position)) * values[position]
            if position >= 1:
                lower = (float(degree - position) - fractions) * values[position - 1]
                term = lower if term is None else term + lower
            updated.append(term * (1.0 / (degree - 1)))
        values = updated
    return values


def pick(selected, weights):
    total = jnp.where(selected == 4, weights[4], 0.0)
    for degree in (3, 2, 1, 0):
        total = jnp.where(selected == degree, weights[degree], total)
    return total


def occupied_rows(count_ref, chunk):
    sub = lax.broadcasted_iota(jnp.int32, (8, 128), 0)
    slot = lax.broadcasted_iota(jnp.int32, (8, 128), 1)
    counts = jnp.zeros((8, 128), jnp.int32)
    for row in range(8):
        counts = jnp.where(sub == row, count_ref[chunk // 2, (chunk % 2) * 8 + row], counts)
    return slot < counts


def prepare(frac_ref, base_ref, wx_ref, wy_ref, wz_ref, charge_of):
    def chunk_step(chunk, carry):
        rows = pl.ds(pl.multiple_of(chunk * 8, 8), 8)
        weights = spline_weights(frac_ref[0, rows, :])
        offset = (base_ref[0, rows, :] & 3) + 4
        charge = charge_of(chunk, rows)
        for position in range(8):
            window = pick(offset - position, weights)
            wx_ref[position, rows, :] = window if charge is None else window * charge
        for degree, weight in enumerate(spline_weights(frac_ref[1, rows, :])):
            wy_ref[degree, rows, :] = weight
        for degree, weight in enumerate(spline_weights(frac_ref[2, rows, :])):
            wz_ref[degree, rows, :] = weight
        return carry

    lax.fori_loop(0, CELLS // 8, chunk_step, 0)


def depth_weights(base_ref, wz_ref, cell):
    row = pl.ds(cell, 1)
    start = (base_ref[2, row, :] - 2) & (NZ - 1)
    block, inside = start >> 5, start & 31
    weights = [wz_ref[degree, row, :] for degree in range(5)]
    level = lax.broadcasted_iota(jnp.int32, (40, 128), 0)
    window = pick(4 - (level - inside), weights)
    high = window.astype(BF).astype(F32)
    low = window - high
    parts = []
    for value in (high, low):
        pieces = []
        for index in range(8):
            here = block == index
            before = block == (index - 1) % 8
            first = jnp.where(here, value[:8], jnp.where(before, value[32:], 0.0))
            rest = jnp.where(here, value[8:32], 0.0)
            pieces += [first, rest]
        parts.append(jnp.concatenate(pieces, axis=0).astype(BF))
    return parts


def pair_depth(base_ref, wz_ref, cell):
    first = depth_weights(base_ref, wz_ref, cell)
    second = depth_weights(base_ref, wz_ref, cell + 1)
    return (
        jnp.concatenate([first[0], second[0]], axis=1),
        jnp.concatenate([first[1], second[1]], axis=1),
    )


def pair_window_y(base_ref, wy_ref, cell):
    parts = []
    for side in (0, 1):
        row = pl.ds(cell + side, 1)
        position = lax.broadcasted_iota(jnp.int32, (16, 128), 0)
        selected = ((base_ref[1, row, :] & 3) + 4 + 4 * side) - position
        parts.append(pick(selected, [wy_ref[degree, row, :] for degree in range(5)]))
    return jnp.concatenate(parts, axis=1)


def pair_row(ref, position, cell):
    return jnp.concatenate(
        [ref[position, pl.ds(cell, 1), :], ref[position, pl.ds(cell + 1, 1), :]], axis=1
    )


def start_all(moves, sems):
    copies = [
        pltpu.make_async_copy(source, target, sems.at[index])
        for index, (source, target) in enumerate(moves)
    ]
    for copy in copies:
        copy.start()
    return copies


def spread_kernel(
    count_hbm,
    cot_hbm,
    frac_hbm,
    base_hbm,
    table_hbm,
    out_hbm,
    count_ref,
    cot_ref,
    frac_ref,
    base_ref,
    table_ref,
    out_ref,
    ext_ref,
    wx_ref,
    wy_ref,
    wz_ref,
    sems,
    out_sems,
):
    copies = start_all(
        [
            (count_hbm, count_ref),
            (cot_hbm, cot_ref),
            (frac_hbm, frac_ref),
            (base_hbm, base_ref),
            (table_hbm, table_ref),
        ],
        sems,
    )

    def clear(step, carry):
        rows = pl.ds(pl.multiple_of(step * EXT_Y, 8), EXT_Y)
        for half in (0, 1):
            ext_ref[half, rows, :] = jnp.zeros((EXT_Y, 128), F32)
        return carry

    lax.fori_loop(0, EXT_X, clear, 0, unroll=4)
    for copy in copies[:4]:
        copy.wait()

    def charge_of(chunk, rows):
        return jnp.where(occupied_rows(count_ref, chunk), cot_ref[rows, :], 0.0)

    prepare(frac_ref, base_ref, wx_ref, wy_ref, wz_ref, charge_of)

    def pair_step(step, carry):
        cell_x, pair = step // 8, step % 8
        cell = step * 2
        depth_high, depth_low = pair_depth(base_ref, wz_ref, cell)
        window_y = pair_window_y(base_ref, wy_ref, cell)
        lifted = jnp.concatenate(
            [pair_row(wx_ref, u, cell) * window_y for u in range(8)], axis=0
        )
        high, low = split(lifted)
        both = dot_nt(jnp.concatenate([high, low], axis=0), depth_high)
        patch = both[:128] + both[128:] + dot_nt(high, depth_low)
        for u in range(8):
            rows = pl.ds(pl.multiple_of((cell_x * 4 + u) * EXT_Y + pair * 8, 8), 16)
            for half in (0, 1):
                ext_ref[half, rows, :] += patch[16 * u : 16 * u + 16, 128 * half : 128 * half + 128]
        return carry

    lax.fori_loop(0, CELLS // 2, pair_step, 0, unroll=8)

    lane = lax.broadcasted_iota(jnp.int32, (128, 128), 1)

    def transform(blocks, first_row):
        high, low = split(jnp.concatenate(blocks, axis=0))
        both = dot_nt(table_ref[...], high)
        planes = both[:256] + both[256:] + dot_nt(table_ref[:256], low)
        for duo in (0, 1):
            first = planes[:128, 128 * duo : 128 * duo + 128]
            second = planes[128:, 128 * duo : 128 * duo + 128]
            left = jnp.where(lane < 64, first, pltpu.roll(second, 64, 1))
            right = jnp.where(lane < 64, pltpu.roll(first, 64, 1), second)
            out_ref[pl.ds(first_row + 2 * duo, 128, stride=ROWS), :] = left
            out_ref[pl.ds(first_row + 2 * duo + 1, 128, stride=ROWS), :] = right

    def send(index):
        rows = pl.ds(8 * index, 8)
        copy = pltpu.make_async_copy(
            out_ref.reshape(DEVICES, ROWS, 128).at[:, rows, :],
            out_hbm.at[:, rows, :],
            out_sems.at[index],
        )
        copy.start()
        return copy

    copies[4].wait()
    sends = []
    for step in range(9):
        blocks = []
        for row in range(4):
            rows = pl.ds((step * 4 + row) * EXT_Y, 64)
            blocks.append(jnp.concatenate([ext_ref[0, rows, :], ext_ref[1, rows, :]], axis=1))
        transform(blocks, step * 4)
        if step % 2 == 1:
            sends.append(send(step // 2))
    blocks = []
    for rim in range(4):
        rows = pl.ds(64 + rim, EXT_X, stride=EXT_Y)
        block = jnp.concatenate([ext_ref.at[0][rows, :], ext_ref.at[1][rows, :]], axis=1)
        blocks.append(jnp.concatenate([block, jnp.zeros((24, 256), F32)], axis=0))
    transform(blocks, 36)
    sends.append(send(4))
    for copy in sends:
        copy.wait()


def sort_kernel(
    flag_ref,
    influence_hbm,
    zero_hbm,
    sort_hbm,
    tables_hbm,
    weight_hbm,
    kept_hbm,
    sort,
    influence,
    zero_plane,
    weight_ref,
    tables,
    sems,
):
    plane, middle = flag_ref[0], flag_ref[1]
    moves = [(sort_hbm, sort)]
    for part in range(4):
        columns = pl.ds(128 * part, 128)
        moves.append((influence_hbm.at[plane, :, columns], influence.at[part]))
        moves.append((zero_hbm.at[:, columns], zero_plane.at[part]))
    moves.append((tables_hbm, tables))
    copies = start_all(moves, sems)
    for copy in copies[:-1]:
        copy.wait()

    def put(first, f, value):
        high, low = split(value)
        value = dot(high, sort[...]) + dot(low, sort[...])
        for residue in range(4):
            weight_ref[first + 4 * f + residue] = value[:, 128 * residue : 128 * residue + 128]

    def plane_rows(planes, f):
        rows = pl.ds(f, 256, stride=2)
        return jnp.concatenate([planes.at[part][rows, :] for part in range(4)], axis=1)

    @pl.when(middle == 0)
    def _plain():
        for f in (0, 1):
            put(0, f, plane_rows(influence, f))
        for which in range(8):
            weight_ref[8 + which] = jnp.zeros((256, 128), F32)

    @pl.when(middle != 0)
    def _mixed():
        for f in (0, 1):
            own, other = plane_rows(influence, f), plane_rows(zero_plane, f)
            put(0, f, (own + other) * 0.5)
            put(8, f, (own - other) * 0.5)

    pltpu.sync_copy(weight_ref, weight_hbm.at[pl.ds(0, 16)])
    copies[-1].wait()
    pltpu.sync_copy(tables, kept_hbm.at[pl.ds(0, TABLE_ROWS), :])


def plane_kernel(
    flag_ref,
    in_ref,
    weight_hbm,
    tables_hbm,
    out_ref,
    weight_ref,
    tables,
    block_high,
    block_low,
    rim_high,
    rim_low,
    spectrum,
    result,
    sems,
):
    middle = flag_ref[1]

    def table_move(first, count):
        rows = pl.ds(first, count)
        return tables_hbm.at[rows, :], tables.at[rows, :]

    moves = [
        table_move(0, Y_ROWS),
        table_move(X_START, X_ROWS),
        (weight_hbm.at[pl.ds(0, 8)], weight_ref.at[pl.ds(0, 8)]),
        table_move(TURN_START, TURN_ROWS),
        (weight_hbm.at[pl.ds(8, 8)], weight_ref.at[pl.ds(8, 8)]),
    ]
    copies = [
        pltpu.make_async_copy(source, target, sems.at[index])
        for index, (source, target) in enumerate(moves)
    ]
    for copy in copies[:3]:
        copy.start()

    @pl.when(middle != 0)
    def _more():
        for copy in copies[3:]:
            copy.start()

    sub = lax.broadcasted_iota(jnp.int32, (8, 128), 0)
    turn_sign = jnp.where(lax.broadcasted_iota(jnp.int32, (32, 128), 1) < 64, -1.0, 1.0)

    def times_i(value):
        return pltpu.roll(value, 64, 1) * turn_sign[: value.shape[0]]

    def block_rows(p, q, first, count):
        return pl.ds((p * PY + q) * ROWS + first, count)

    def rim_rows(p):
        tiles = []
        for q in range(0, PY, 2):
            even = in_ref[block_rows(p, q, 32, 8), :]
            odd = in_ref[block_rows(p, q + 1, 32, 8), :]
            tiles.append(jnp.where(sub < 4, pltpu.roll(even, 4, 0), odd))
        tiles.append(jnp.zeros((96, 128), F32))
        return jnp.concatenate(tiles, axis=0).T

    def main_rows(p, q):
        own = in_ref[block_rows(p, q, 0, 32), :]
        edge = in_ref[block_rows((p + PX - 1) % PX, q, 32, 8), :]
        return jnp.concatenate([own[:8] + jnp.where(sub < 4, edge, 0.0), own[8:]], axis=0)

    turned_rims = {p: rim_rows(p) for p in (7, 15)}

    def edge_rows(p):
        before = turned_rims[(p + PX - 1) % PX]
        if p not in turned_rims:
            turned_rims[p] = rim_rows(p)
        turned = turned_rims[p]
        own = turned[0:32] + pltpu.roll(turned[64:96], 32, 1)
        edge = before[32:40] + pltpu.roll(before[96:104], 32, 1)
        first = own[:8] + jnp.where(sub < 4, edge, 0.0)
        return jnp.concatenate([first, own[8:]], axis=0)

    for p in range(8):
        rows = pl.ds(p * 32, 32)
        for q in range(2):
            columns = pl.ds(128 * q, 128)
            near = [main_rows(p, 2 * t + q) for t in range(4)]
            far = [main_rows(p + 8, 2 * t + q) for t in range(4)]
            for f, sign in ((0, 1.0), (1, -1.0)):
                a = [x + sign * y for x, y in zip(near, far)]
                sum_even, sum_odd = a[0] + a[2], a[1] + a[3]
                diff_even, diff_odd = a[0] - a[2], times_i(a[1] - a[3])
                parts = (
                    sum_even + sum_odd,
                    diff_even - diff_odd,
                    sum_even - sum_odd,
                    diff_even + diff_odd,
                )
                for residue, value in enumerate(parts):
                    high, low = split(value)
                    block_high[4 * f + residue, rows, columns] = high
                    block_low[4 * f + residue, rows, columns] = low
        near, far = edge_rows(p), edge_rows(p + 8)
        for f, value in ((0, near + far), (1, near - far)):
            rim_high[f, rows, :], rim_low[f, rows, :] = split(value)

    def y_table(residue, part):
        return tables[pl.ds((2 * residue + part) * 384, 384), :]

    def x_table(index):
        return pl.ds(X_START + 1024 * index, 1024)

    def left_products(rows, value):
        table = tables[rows, :]
        high, low = split(value)
        both = dot(table, high)
        total = both[:512] + both[512:] + dot(table[:512], low)
        return total[:256], total[256:]

    blocks = [(f, residue) for f in (0, 1) for residue in range(4)]
    copies[0].wait()
    copies[1].wait()
    for f, residue in blocks:
        which = 4 * f + residue
        high = jnp.concatenate([block_high[which], rim_high[f]], axis=1)
        low = jnp.concatenate([block_low[which], rim_low[f]], axis=1)
        both = dot(jnp.concatenate([high, low], axis=0), y_table(residue, 0))
        along_y = both[:256] + both[256:] + dot(high, y_table(residue, 1))
        cosine, sine = left_products(x_table(f), along_y)
        spectrum[which, :, :128] = cosine[:, :128] + sine[:, 128:]
        spectrum[which, :, 128:] = cosine[:, 128:] - sine[:, :128]

    copies[2].wait()

    @pl.when(middle == 0)
    def _scale():
        for which in range(8):
            for part in (0, 1):
                spectrum[which, :, pl.ds(128 * part, 128)] *= weight_ref[which]

    @pl.when(middle != 0)
    def _scale_mixed():
        copies[3].wait()
        copies[4].wait()
        for f in (0, 1):
            left = tables[pl.ds(TURN_START + 256 * f, 256), :]
            turned = []
            for residue in range(4):
                right = tables[pl.ds(TURN_START + 512 + 256 * (residue > 0), 256), :]
                high, low = split(spectrum[4 * f + (4 - residue) % 4])
                high, low = split(dot(left, high) + dot(left, low))
                turned.append(dot(high, right) + dot(low, right))
            for residue in range(4):
                which = 4 * f + residue
                for part, sign in ((0, 1.0), (1, -1.0)):
                    columns = pl.ds(128 * part, 128)
                    spectrum[which, :, columns] = (
                        spectrum[which, :, columns] * weight_ref[which]
                        + sign * turned[residue][:, 128 * part : 128 * part + 128] * weight_ref[8 + which]
                    )

    for f, residue in blocks:
        which = 4 * f + residue
        cosine, sine = left_products(x_table(2 * f), spectrum[which])
        back = jnp.concatenate(
            [cosine[:, :128] - sine[:, 128:], cosine[:, 128:] + sine[:, :128]], axis=1
        )
        high, low = split(back)
        both = dot_nt(jnp.concatenate([high, low], axis=0), y_table(residue, 0))
        result[which] = both[:256] + both[256:] + dot_nt(high, y_table(residue, 1))

    def chunk_copy(p):
        rows = pl.ds(p * PY * ROWS, PY * ROWS)
        return pltpu.make_async_copy(out_ref.at[rows, :], out_hbm.at[rows, :], out_sems.at[p])

    def quarters(first, count, columns):
        found = []
        for f in (0, 1):
            a = [result[4 * f + residue, pl.ds(first, count), columns] for residue in range(4)]
            sum_even, sum_odd = a[0] + a[2], a[1] + a[3]
            diff_even, diff_odd = a[0] - a[2], times_i(a[1] - a[3])
            found.append(
                (
                    sum_even + sum_odd,
                    diff_even + diff_odd,
                    sum_even - sum_odd,
                    diff_even - diff_odd,
                )
            )
        return found

    def total(first, count):
        rows, columns = pl.ds(first, count), pl.ds(256, 128)
        return [
            (result[4 * f, rows, columns] + result[4 * f + 1, rows, columns])
            + (result[4 * f + 2, rows, columns] + result[4 * f + 3, rows, columns])
            for f in (0, 1)
        ]

    for p in range(8):
        first, after = p * 32, ((p + 1) % 8) * 32
        wrap = -1.0 if p == 7 else 1.0
        own, edge = total(first, 32), total(after, 8)
        rims = []
        for sign in (1.0, -1.0):
            tall = jnp.concatenate(
                [own[0] + sign * own[1], edge[0] + (sign * wrap) * edge[1], jnp.zeros((88, 128), F32)],
                axis=0,
            ).T
            rims.append(tall[0:32] + pltpu.roll(tall[32:64], 64, 1))
        for q in range(2):
            columns = pl.ds(128 * q, 128)
            own, edge = quarters(first, 32, columns), quarters(after, 8, columns)
            for t in range(4):
                target_q = 2 * t + q
                for far, sign in ((0, 1.0), (8, -1.0)):
                    target_p = p + far
                    out_ref[block_rows(target_p, target_q, 0, 32), :] = own[0][t] + sign * own[1][t]
                    x_rim = edge[0][t] + (sign * wrap) * edge[1][t]
                    tile = rims[far // 8][8 * (target_q // 2) : 8 * (target_q // 2) + 8]
                    if target_q % 2 == 0:
                        tile = pltpu.roll(tile, 4, 0)
                    out_ref[block_rows(target_p, target_q, 32, 8), :] = jnp.where(
                        sub < 4, x_rim, tile
                    )


def atoms_kernel(
    frac_hbm,
    base_hbm,
    table_hbm,
    depth_ref,
    window_out,
    frac_ref,
    base_ref,
    table_ref,
    wx_ref,
    wy_ref,
    wz_ref,
    sems,
):
    step = pl.program_id(0)

    @pl.when(step == 0)
    def _first():
        moves = [(frac_hbm, frac_ref), (base_hbm, base_ref), (table_hbm, table_ref)]
        for copy in start_all(moves, sems):
            copy.wait()
        prepare(frac_ref, base_ref, wx_ref, wy_ref, wz_ref, lambda chunk, rows: None)

    def pair_step(index, carry):
        cell = step * 16 + index * 2
        high, low = pair_depth(base_ref, wz_ref, cell)
        both = dot(table_ref[...], high)
        depth_ref[index, 0], depth_ref[index, 1] = split(
            both[:256] + both[256:] + dot(table_ref[:256], low)
        )
        window_out[index, pl.ds(8, 16), :] = pair_window_y(base_ref, wy_ref, cell)
        for u in range(8):
            window_out[index, pl.ds(u, 1), :] = pair_row(wx_ref, u, cell)
        return carry

    lax.fori_loop(0, 8, pair_step, 0, unroll=2)


def gather_kernel(
    count_hbm,
    in_ref,
    depth_hbm,
    window_hbm,
    out_ref,
    count_ref,
    depth_ref,
    window_ref,
    ext_ref,
    sems,
):
    moves = [(count_hbm, count_ref), (window_hbm.at[pl.ds(0, CELLS // 2)], window_ref)]
    for row in range(8):
        pairs = pl.ds(8 * row, 8)
        moves.append((depth_hbm.at[pairs], depth_ref.at[pairs]))
    copies = start_all(moves, sems)

    def turned(row):
        block = in_ref[pl.ds(row, 128, stride=ROWS), :].T
        return block[:64], block[64:]

    def row_step(row, carry):
        rows = pl.ds(pl.multiple_of(row * EXT_Y, 8), 64)
        last = pl.ds(pl.multiple_of(row * EXT_Y + 64, 8), 8)
        first, second = turned(row)
        ext_ref[0, rows, :] = first
        ext_ref[1, rows, :] = second
        for half in (0, 1):
            ext_ref[half, last, :] = jnp.zeros((8, 128), F32)
        return carry

    lax.fori_loop(0, 36, row_step, 0, unroll=6)
    for rim in range(4):
        rows = pl.ds(64 + rim, EXT_X, stride=EXT_Y)
        first, second = turned(36 + rim)
        ext_ref.at[0][rows, :] = first[:EXT_X]
        ext_ref.at[1][rows, :] = second[:EXT_X]
    for copy in copies[:2]:
        copy.wait()

    def pair_work(cell_x, pair):
        index = cell_x * 8 + pair
        windows = []
        for u in range(8):
            rows = pl.ds(pl.multiple_of((cell_x * 4 + u) * EXT_Y + pair * 8, 8), 16)
            windows.append(jnp.concatenate([ext_ref[0, rows, :], ext_ref[1, rows, :]], axis=1))
        high, low = split(jnp.concatenate(windows, axis=0))
        both = dot(jnp.concatenate([high, low], axis=0), depth_ref[index, 0])
        part = both[:128] + both[128:] + dot(high, depth_ref[index, 1])
        total = part[:16] * window_ref[index, pl.ds(0, 1), :]
        for u in range(1, 8):
            total += part[16 * u : 16 * u + 16] * window_ref[index, pl.ds(u, 1), :]
        total = jnp.sum(total * window_ref[index, pl.ds(8, 16), :], axis=0, keepdims=True)
        out_ref[pl.ds(index * 2, 1), :] = total[:, :128]
        out_ref[pl.ds(index * 2 + 1, 1), :] = total[:, 128:]

    for cell_x in range(8):
        copies[2 + cell_x].wait()
        for pair in range(8):
            pair_work(cell_x, pair)

    def mask_step(chunk, carry):
        rows = pl.ds(pl.multiple_of(chunk * 8, 8), 8)
        out_ref[rows, :] = jnp.where(occupied_rows(count_ref, chunk), out_ref[rows, :], 0.0)
        return carry

    lax.fori_loop(0, CELLS // 8, mask_step, 0, unroll=2)


VMEM = pl.BlockSpec(memory_space=pltpu.VMEM)
SMEM = pl.BlockSpec(memory_space=pltpu.SMEM)
HBM = pl.BlockSpec(memory_space=pltpu.HBM)
MIB = 1024 * 1024


def scratch(shape, dtype=F32):
    return pltpu.VMEM(shape, dtype)


def dmas(count):
    return pltpu.SemaphoreType.DMA((count,))


def params(mib):
    return pltpu.CompilerParams(vmem_limit_bytes=mib * MIB)


def cost(flops):
    return pl.CostEstimate(flops=flops, bytes_accessed=10**7, transcendentals=0)


ATOMS = (3, CELLS, 128)
WEIGHTS = [scratch((8, CELLS, 128)), scratch((5, CELLS, 128)), scratch((5, CELLS, 128))]
EXTENDED = scratch((2, EXT_X * EXT_Y, 128))


def per_device(cotangent, fraction, grid_base, cell_count, influence):
    device = lax.axis_index("px") * PY + lax.axis_index("py")
    flags = jnp.stack([(device < MIDDLE).astype(jnp.int32), (device == MIDDLE).astype(jnp.int32)])
    zero_plane = lax.ppermute(influence[0], ("px", "py"), [(0, MIDDLE)])
    fraction = fraction.reshape(ATOMS)
    grid_base = grid_base.reshape(ATOMS)
    forward_z, inverse_z = depth_tables()

    sent = pl.pallas_call(
        spread_kernel,
        out_shape=jax.ShapeDtypeStruct((DEVICES, ROWS, 128), F32),
        in_specs=[HBM] * 5,
        out_specs=HBM,
        scratch_shapes=[
            pltpu.SMEM((8, 16), jnp.int32),
            scratch((CELLS, 128)),
            scratch(ATOMS),
            scratch(ATOMS, jnp.int32),
            scratch((512, 256), BF),
            scratch((DEVICES * ROWS, 128)),
            EXTENDED,
            *WEIGHTS,
            dmas(5),
            dmas(5),
        ],
        compiler_params=params(62),
        cost_estimate=cost(10**10),
        name="spread",
    )(cell_count, cotangent.reshape(CELLS, 128), fraction, grid_base, forward_z)

    def exchange(array):
        return lax.all_to_all(array, ("px", "py"), split_axis=0, concat_axis=0, tiled=True)

    sent, zero_plane, fraction, grid_base = lax.optimization_barrier(
        (sent, zero_plane, fraction, grid_base)
    )
    planes = exchange(sent).reshape(DEVICES * ROWS, 128)
    weight, tables = pl.pallas_call(
        sort_kernel,
        out_shape=(
            jax.ShapeDtypeStruct((136, 256, 128), F32),
            jax.ShapeDtypeStruct((34816, 256), BF),
        ),
        in_specs=[SMEM] + [HBM] * 4,
        out_specs=(HBM, HBM),
        scratch_shapes=[
            scratch((512, 512), BF),
            scratch((4, 512, 128)),
            scratch((4, 512, 128)),
            scratch((16, 256, 128)),
            scratch((TABLE_ROWS, 256), BF),
            dmas(10),
        ],
        compiler_params=params(56),
        cost_estimate=cost(10**9),
        name="sort_influence",
    )(flags, influence, zero_plane, sort_table(), plane_tables())

    pairs = CELLS // 2
    depth, window = pl.pallas_call(
        atoms_kernel,
        grid=(8,),
        out_shape=(
            jax.ShapeDtypeStruct((pairs, 2, 256, 256), BF),
            jax.ShapeDtypeStruct((704, 24, 256), F32),
        ),
        in_specs=[HBM] * 3,
        out_specs=(
            pl.BlockSpec((8, 2, 256, 256), lambda i: (i, 0, 0, 0)),
            pl.BlockSpec((8, 24, 256), lambda i: (i, 0, 0)),
        ),
        scratch_shapes=[
            scratch(ATOMS),
            scratch(ATOMS, jnp.int32),
            scratch((512, 256), BF),
            *WEIGHTS,
            dmas(3),
        ],
        compiler_params=params(56),
        cost_estimate=cost(10**10),
        name="atoms",
    )(fraction, grid_base, inverse_z)

    planes, depth, window = lax.optimization_barrier((planes, depth, window))
    back = pl.pallas_call(
        plane_kernel,
        out_shape=jax.ShapeDtypeStruct((DEVICES * ROWS, 128), F32),
        in_specs=[SMEM, VMEM, HBM, HBM],
        out_specs=VMEM,
        scratch_shapes=[
            scratch((16, 256, 128)),
            scratch((TABLE_ROWS, 256), BF),
            scratch((8, 256, 256), BF),
            scratch((8, 256, 256), BF),
            scratch((2, 256, 128), BF),
            scratch((2, 256, 128), BF),
            scratch((8, 256, 256)),
            scratch((8, 256, 384)),
            dmas(5),
        ],
        compiler_params=params(48),
        name="planes",
    )(flags, planes, weight, tables)
    returned = exchange(back.reshape(DEVICES, ROWS, 128)).reshape(DEVICES * ROWS, 128)

    gradient = pl.pallas_call(
        gather_kernel,
        out_shape=jax.ShapeDtypeStruct((CELLS, 128), F32),
        in_specs=[HBM, VMEM, HBM, HBM],
        out_specs=VMEM,
        scratch_shapes=[
            pltpu.SMEM((8, 16), jnp.int32),
            scratch((pairs, 2, 256, 256), BF),
            scratch((pairs, 24, 256)),
            EXTENDED,
            dmas(10),
        ],
        compiler_params=params(48),
        name="gather",
    )(cell_count, returned, depth, window)
    return gradient.reshape(cotangent.shape)


def solution(mesh):
    placed = (
        P("px", "py", None),
        P(None, "px", "py", None),
        P(None, "px", "py", None),
        P("px", "py"),
        P(("px", "py"), None, None),
    )
    return jax.shard_map(
        per_device, mesh=mesh, in_specs=placed, out_specs=P("px", "py", None), check_vma=False
    )
```

time: 170 us -> 123 us (0.72)
  waiting for transfers between devices: 34.9 us -> 10.8 us
  Pallas kernels: 77.1 us -> 55.9 us
  local copies, waits for them, and re-layouts: 3.81 us -> 1.3 us
    all_to_all x1, waiting for transfers between devices: 34.9 us -> 10.8 us  [exchange(): lax.all_to_all(array, ('px', 'py'), split_axis=0, concat_axis=0, tiled=True)]
    pallas_call x1, Pallas kernels: 27.3 us -> 7.98 us  [per_device(): pl.pallas_call(gather_kernel, out_shape=jax.ShapeDtypeStruct((CELLS, 128)...]
    pallas_call x1, Pallas kernels: 21.3 us -> 11.7 us  [per_device(): pl.pallas_call(plane_kernel, out_shape=jax.ShapeDtypeStruct((DEVICES * RO...]
    pallas_call x1 -> x3, Pallas kernels: 28.5 us -> 36.2 us  [the longest x1 17.9 us: per_device(): pl.pallas_call(atoms_kernel, grid=(8,), out_shape=(jax.ShapeDtypeStruct((...]
    unnamed x4, local copies, waits for them, and re-layouts: 2.52 us -> 0.01 us
  transfers between devices with their start and end apart: 2 -> 2, of which waited for: 1 -> 1; matrix products, arithmetic and copies ran while one was open for 0% -> 0% of each run, Pallas kernels for 17% -> 30%
where the time goes in v2:
time: 123 us; the launch traced here: 122 us
  Pallas kernels  55.9 us (45%)
  blocking collectives  40.3 us (33%)
  starting transfers between devices  12.8 us (10%)
  waiting for transfers between devices  10.8 us (9%)
  local copies, waits for them, and re-layouts  1.3 us (1%)
    all_to_all x1, blocking collectives, exchange(): lax.all_to_all(array, ('px', 'py'), split_axis=0, concat_axis=0, tiled=True)  40.3 us
    pallas_call x1, Pallas kernels, per_device(): pl.pallas_call(atoms_kernel, grid=(8,), out_shape=(jax.ShapeDtypeStruct((...  17.9 us
    pallas_call x1, Pallas kernels, per_device(): pl.pallas_call(spread_kernel, out_shape=jax.ShapeDtypeStruct((DEVICES, RO...  12 us
    pallas_call x1, Pallas kernels, per_device(): pl.pallas_call(plane_kernel, out_shape=jax.ShapeDtypeStruct((DEVICES * RO...  11.7 us
    all_to_all x1, waiting for transfers between devices, exchange(): lax.all_to_all(array, ('px', 'py'), split_axis=0, concat_axis=0, tiled=True)  10.8 us
    pallas_call x1, Pallas kernels, per_device(): pl.pallas_call(gather_kernel, out_shape=jax.ShapeDtypeStruct((CELLS, 128)...  7.98 us
    ppermute x1, starting transfers between devices, per_device(): zero_plane = lax.ppermute(influence[0], ('px', 'py'), [(0, MIDDLE)])  6.85 us
    pallas_call x1, Pallas kernels, per_device(): pl.pallas_call(sort_kernel, out_shape=(jax.ShapeDtypeStruct((136, 256, 12...  6.31 us
  transfers between devices with their start and end apart: 2, of which 1 were waited for; matrix products, arithmetic and copies ran while one was open for 0% of the time, Pallas kernels for 30%

profile of v2, /device:TPU:0, one launch (start us, length us, event | category | flops | bytes accessed | tf_op | source)
XLA Modules:
  0.0 121.9 jit_solution(2548402319709027254)
XLA Ops:
  0.0 1.3 %slice_bitcast_fusion = f32[512,512]{1,0:T(8,128)S(1)} fusion(f32[2,512,512]{2,1,0:T(8,128)} %influence_hbm.1), kind=kLoop, calls=%fused_computation | loop fusion | bytes 2097152 | tf_op jit(solution)/shard_map/squeeze | solution.py:747
  1.3 6.9 %collective-permute-start = (f32[512,512]{1,0:T(8,128)S(1)}, f32[512,512]{1,0:T(8,128)}, u32[]{:S(2)}, u32[]{:S(2)}) collective-permute-start(f32[512,512]{1,0:T(8,128)S(1)} %slice_bitcast_fusion), channel_id=1, source_target_pairs={{0,64}} | collective-permute-start | bytes 3145736 | tf_op jit(solution)/shard_map/ppermute | solution.py:747
  8.2 12.0 %spread.1 = f32[128,40,128]{2,1,0:T(8,128)} custom-call(s32[8,16]{1,0:T(8,128)} %count_hbm.3, f32[128,128]{1,0:T(8,128)} %bitcast.18, f32[3,128,128]{2,1,0:T(8,128)} %bitcast.14, s32[3,128,128]{2,1,0:T(8,128)} %bitcast.16, bf16[512,256]{1,0:T(8,128)(2,1)} %constant.21.clone.table_hbm), custom_call_target="tpu_custom_call" | custom-call | flops 10000000000 | bytes 10000000 | tf_op jit(solution)/shard_map/spread/pallas_call | solution.py:752
  20.1 0.0 collective-permute-done.zero_hbm
  20.2 5.9 %all-to-all-start = ((f32[128,40,128]{2,1,0:T(8,128)}), f32[128,40,128]{2,1,0:T(8,128)S(1)}, u32[]{:S(2)}, u32[]{:S(2)}) async-start(f32[128,40,128]{2,1,0:T(8,128)} %spread.1), calls=%async_computation | async-start | bytes 5242880 | tf_op jit(solution)/shard_map/all_to_all | solution.py:775
  26.1 0.6 add_convert_fusion.flag_ref
  26.7 6.3 %sort_influence.1 = (f32[136,256,128]{2,1,0:T(8,128)}, bf16[34816,256]{1,0:T(8,128)(2,1)}) custom-call(s32[2]{0:T(128)} %add_convert_fusion.flag_ref, f32[2,512,512]{2,1,0:T(8,128)} %influence_hbm.1, f32[512,512]{1,0:T(8,128)} %collective-permute-done.zero_hbm, bf16[512,512]{1,0:T(8,128)(2,1)} %constant.22.clone.sort_hbm, ...), custom_call_target="tpu_custom_call" | custom-call | flops 1000000000 | bytes 10000000 | tf_op jit(solution)/shard_map/sort_influence/pallas_call | solution.py:781
  33.0 0.0 copy-start.1
  33.0 17.9 %atoms.1 = (bf16[64,2,256,256]{3,2,1,0:T(8,128)(2,1)}, f32[704,24,256]{2,1,0:T(8,128)}) custom-call(f32[3,128,128]{2,1,0:T(8,128)} %bitcast.15, s32[3,128,128]{2,1,0:T(8,128)} %bitcast.17, bf16[512,256]{1,0:T(8,128)(2,1)} %constant.24.clone.table_hbm), custom_call_target="tpu_custom_call" | custom-call | flops 10000000000 | bytes 10000000 | tf_op jit(solution)/shard_map/atoms/pallas_call | solution.py:803
  50.9 10.8 %all-to-all-done = f32[128,40,128]{2,1,0:T(8,128)S(1)} async-done(((f32[128,40,128]{2,1,0:T(8,128)}), f32[128,40,128]{2,1,0:T(8,128)S(1)}, u32[]{:S(2)}, u32[]{:S(2)}) %all-to-all-start) | async-done | bytes 2621472 | tf_op jit(solution)/shard_map/all_to_all | solution.py:775
  61.7 0.0 copy-done.1
  61.7 11.7 %planes.1 = f32[5120,128]{1,0:T(8,128)S(1)} custom-call(s32[2]{0:T(128)S(1)} %copy-done.1, f32[5120,128]{1,0:T(8,128)S(1)} %bitcast.12, f32[136,256,128]{2,1,0:T(8,128)} %get-tuple-element.23.weight_hbm, bf16[34816,256]{1,0:T(8,128)(2,1)} %get-tuple-element.24.tables_hbm), custom_call_target="tpu_custom_call" | custom-call | tf_op jit(solution)/shard_map/planes/pallas_call | solution.py:828
  73.4 0.0 copy-start
  73.5 40.3 %all_to_all.10 = f32[128,40,128]{2,1,0:T(8,128)S(1)} all-to-all(f32[128,40,128]{2,1,0:T(8,128)S(1)} %bitcast.13), channel_id=1, replica_groups=mesh['px'=16,'py'=8] {'px','py'}, dimensions={0} | all-to-all | bytes 5242880 | tf_op jit(solution)/shard_map/all_to_all | solution.py:775
  113.8 0.0 copy-done
  113.8 8.0 %gather.1 = f32[128,128]{1,0:T(8,128)} custom-call(s32[8,16]{1,0:T(8,128)S(1)} %copy-done, f32[5120,128]{1,0:T(8,128)S(1)} %bitcast.11, bf16[64,2,256,256]{3,2,1,0:T(8,128)(2,1)} %get-tuple-element.25.depth_hbm, f32[704,24,256]{2,1,0:T(8,128)} %get-tuple-element.26.window_hbm), custom_call_target="tpu_custom_call" | custom-call | tf_op jit(solution)/shard_map/gather/pallas_call | solution.py:849
Async XLA Ops:
  1.3 18.8 %collective-permute-start = (f32[512,512]{1,0:T(8,128)S(1)}, f32[512,512]{1,0:T(8,128)}, u32[]{:S(2)}, u32[]{:S(2)}) collective-permute-start(f32[512,512]{1,0:T(8,128)S(1)} %slice_bitcast_fusion), channel_id=1, source_target_pairs={{0,64}} | collective-permute-start | bytes 3145736 | tf_op jit(solution)/shard_map/ppermute | solution.py:747
  20.2 41.5 %all-to-all-start = ((f32[128,40,128]{2,1,0:T(8,128)}), f32[128,40,128]{2,1,0:T(8,128)S(1)}, u32[]{:S(2)}, u32[]{:S(2)}) async-start(f32[128,40,128]{2,1,0:T(8,128)} %spread.1), calls=%async_computation | async-start | bytes 5242880 | tf_op jit(solution)/shard_map/all_to_all | solution.py:775
  33.0 28.7 %copy-start.1 = (s32[2]{0:T(128)S(1)}, s32[2]{0:T(128)}, u32[]{:S(2)}) copy-start(s32[2]{0:T(128)} %add_convert_fusion.flag_ref) | copy-start | bytes 28
  73.4 40.4 %copy-start = (s32[8,16]{1,0:T(8,128)S(1)}, s32[8,16]{1,0:T(8,128)}, u32[]{:S(2)}) copy-start(s32[8,16]{1,0:T(8,128)} %count_hbm.3) | copy-start | bytes 1540

commit v3 on v2

--- a/solution.py
+++ b/solution.py
@@ -1,3 +1,5 @@
+import functools
+
 import jax
 import jax.numpy as jnp
 import ml_dtypes
@@ -14,6 +16,9 @@
 CELLS = 128
 ROWS = 40
 EXT_X, EXT_Y = 40, 72
+HALF_ROWS = 264
+ATOM_CALLS = ((0, 2, 16), (2, 2, 16), (4, 4, 80))
+ATOM_PARTS = len(ATOM_CALLS)
 BF, F32 = jnp.bfloat16, jnp.float32
 
 
@@ -163,50 +168,72 @@
     lax.fori_loop(0, CELLS // 8, chunk_step, 0)
 
 
-def depth_weights(base_ref, wz_ref, cell):
-    row = pl.ds(cell, 1)
-    start = (base_ref[2, row, :] - 2) & (NZ - 1)
+def cell_rows(ref, index, cell_x, cell_y):
+    first = pl.multiple_of(cell_x * 16 + cell_y // 8 * 8, 8)
+    return ref[index, pl.ds(first, 8), :][cell_y % 8 : cell_y % 8 + 1]
+
+
+def depth_weights(base_ref, wz_ref, cell_x, cell_y):
+    start = jnp.broadcast_to((cell_rows(base_ref, 2, cell_x, cell_y) - 2) & (NZ - 1), (8, 128))
     block, inside = start >> 5, start & 31
-    weights = [wz_ref[degree, row, :] for degree in range(5)]
-    level = lax.broadcasted_iota(jnp.int32, (40, 128), 0)
-    window = pick(4 - (level - inside), weights)
-    high = window.astype(BF).astype(F32)
-    low = window - high
+    weights = [
+        jnp.broadcast_to(cell_rows(wz_ref, degree, cell_x, cell_y), (8, 128)) for degree in range(5)
+    ]
+    first = 4 + inside - lax.broadcasted_iota(jnp.int32, (8, 128), 0)
+    highs, lows = [], []
+    for step in range(5):
+        window = pick(first - 8 * step, weights)
+        high = window.astype(BF).astype(F32)
+        highs.append(high)
+        lows.append(window - high)
     parts = []
-    for value in (high, low):
+    zero = jnp.zeros((8, 128), F32)
+    packed = []
+    for value in (highs, lows):
+        packed.append(
+            [
+                jnp.concatenate([value[0], value[1]], axis=0).astype(BF),
+                jnp.concatenate([value[2], value[3]], axis=0).astype(BF),
+                jnp.concatenate([value[4], zero], axis=0).astype(BF),
+            ]
+        )
+    one = jnp.ones((8, 128), F32)
+    hot = []
+    for index in range(8):
+        mark = jnp.where(block == index, one, 0.0)
+        hot.append(jnp.concatenate([mark, mark], axis=0).astype(BF))
+    for value in packed:
         pieces = []
         for index in range(8):
-            here = block == index
-            before = block == (index - 1) % 8
-            first = jnp.where(here, value[:8], jnp.where(before, value[32:], 0.0))
-            rest = jnp.where(here, value[8:32], 0.0)
-            pieces += [first, rest]
-        parts.append(jnp.concatenate(pieces, axis=0).astype(BF))
+            pieces.append(value[0] * hot[index] + value[2] * hot[(index - 1) % 8])
+            pieces.append(value[1] * hot[index])
+        parts.append(jnp.concatenate(pieces, axis=0))
     return parts
 
 
-def pair_depth(base_ref, wz_ref, cell):
-    first = depth_weights(base_ref, wz_ref, cell)
-    second = depth_weights(base_ref, wz_ref, cell + 1)
+def pair_depth(base_ref, wz_ref, cell_x, pair):
+    first = depth_weights(base_ref, wz_ref, cell_x, 2 * pair)
+    second = depth_weights(base_ref, wz_ref, cell_x, 2 * pair + 1)
     return (
         jnp.concatenate([first[0], second[0]], axis=1),
         jnp.concatenate([first[1], second[1]], axis=1),
     )
 
 
-def pair_window_y(base_ref, wy_ref, cell):
+def pair_window_y(base_ref, wy_ref, cell_x, pair):
     parts = []
     for side in (0, 1):
-        row = pl.ds(cell + side, 1)
+        cell_y = 2 * pair + side
         position = lax.broadcasted_iota(jnp.int32, (16, 128), 0)
-        selected = ((base_ref[1, row, :] & 3) + 4 + 4 * side) - position
-        parts.append(pick(selected, [wy_ref[degree, row, :] for degree in range(5)]))
+        selected = ((cell_rows(base_ref, 1, cell_x, cell_y) & 3) + 4 + 4 * side) - position
+        weights = [cell_rows(wy_ref, degree, cell_x, cell_y) for degree in range(5)]
+        parts.append(pick(selected, weights))
     return jnp.concatenate(parts, axis=1)
 
 
-def pair_row(ref, position, cell):
+def pair_row(ref, position, cell_x, pair):
     return jnp.concatenate(
-        [ref[position, pl.ds(cell, 1), :], ref[position, pl.ds(cell + 1, 1), :]], axis=1
+        [cell_rows(ref, position, cell_x, 2 * pair + side) for side in (0, 1)], axis=1
     )
 
 
@@ -266,13 +293,11 @@
 
     prepare(frac_ref, base_ref, wx_ref, wy_ref, wz_ref, charge_of)
 
-    def pair_step(step, carry):
-        cell_x, pair = step // 8, step % 8
-        cell = step * 2
-        depth_high, depth_low = pair_depth(base_ref, wz_ref, cell)
-        window_y = pair_window_y(base_ref, wy_ref, cell)
+    def pair_work(cell_x, pair):
+        depth_high, depth_low = pair_depth(base_ref, wz_ref, cell_x, pair)
+        window_y = pair_window_y(base_ref, wy_ref, cell_x, pair)
         lifted = jnp.concatenate(
-            [pair_row(wx_ref, u, cell) * window_y for u in range(8)], axis=0
+            [pair_row(wx_ref, u, cell_x, pair) * window_y for u in range(8)], axis=0
         )
         high, low = split(lifted)
         both = dot_nt(jnp.concatenate([high, low], axis=0), depth_high)
@@ -281,9 +306,13 @@
             rows = pl.ds(pl.multiple_of((cell_x * 4 + u) * EXT_Y + pair * 8, 8), 16)
             for half in (0, 1):
                 ext_ref[half, rows, :] += patch[16 * u : 16 * u + 16, 128 * half : 128 * half + 128]
+
+    def cell_step(cell_x, carry):
+        for pair in range(8):
+            pair_work(cell_x, pair)
         return carry
 
-    lax.fori_loop(0, CELLS // 2, pair_step, 0, unroll=8)
+    lax.fori_loop(0, 8, cell_step, 0)
 
     lane = lax.broadcasted_iota(jnp.int32, (128, 128), 1)
 
@@ -350,38 +379,50 @@
     for part in range(4):
         columns = pl.ds(128 * part, 128)
         moves.append((influence_hbm.at[plane, :, columns], influence.at[part]))
-        moves.append((zero_hbm.at[:, columns], zero_plane.at[part]))
+        moves.append((zero_hbm.at[:, columns], zero_plane.at[part, pl.ds(0, HALF_ROWS), :]))
     moves.append((tables_hbm, tables))
     copies = start_all(moves, sems)
-    for copy in copies[:-1]:
+    for copy in copies:
         copy.wait()
 
-    def put(first, f, value):
+    def sorted_rows(planes, f, count):
+        rows = pl.ds(f, 256, stride=2)
+        value = jnp.concatenate([planes.at[part][rows, :] for part in range(4)], axis=1)
+        if count < 256:
+            value = jnp.where(lax.broadcasted_iota(jnp.int32, value.shape, 0) < count, value, 0.0)
         high, low = split(value)
-        value = dot(high, sort[...]) + dot(low, sort[...])
-        for residue in range(4):
-            weight_ref[first + 4 * f + residue] = value[:, 128 * residue : 128 * residue + 128]
-
-    def plane_rows(planes, f):
-        rows = pl.ds(f, 256, stride=2)
-        return jnp.concatenate([planes.at[part][rows, :] for part in range(4)], axis=1)
+        return dot(high, sort[...]) + dot(low, sort[...])
 
     @pl.when(middle == 0)
     def _plain():
         for f in (0, 1):
-            put(0, f, plane_rows(influence, f))
+            own = sorted_rows(influence, f, 256)
+            for residue in range(4):
+                weight_ref[4 * f + residue] = own[:, 128 * residue : 128 * residue + 128]
         for which in range(8):
             weight_ref[8 + which] = jnp.zeros((256, 128), F32)
 
     @pl.when(middle != 0)
     def _mixed():
+        index = lax.broadcasted_iota(jnp.int32, (256, 128), 0)
         for f in (0, 1):
-            own, other = plane_rows(influence, f), plane_rows(zero_plane, f)
-            put(0, f, (own + other) * 0.5)
-            put(8, f, (own - other) * 0.5)
+            own = sorted_rows(influence, f, 256)
+            half = sorted_rows(zero_plane, f, HALF_ROWS // 2)
+            left = tables[pl.ds(TURN_START + 256 * f, 256), :]
+            high, low = split(half)
+            high, low = split(dot(left, high) + dot(left, low))
+            for residue in range(4):
+                which = 4 * f + residue
+                columns = slice(128 * residue, 128 * residue + 128)
+                other = (4 - residue) % 4
+                partner = slice(128 * other, 128 * other + 128)
+                right = tables[pl.ds(TURN_START + 512 + 256 * (residue > 0), 128), :][:, :128]
+                turned = dot(high[:, partner], right) + dot(low[:, partner], right)
+                whole = jnp.where(index <= 128 - f, half[:, columns], turned)
+                weight_ref[which] = (own[:, columns] + whole) * 0.5
+                weight_ref[8 + which] = (own[:, columns] - whole) * 0.5
 
     pltpu.sync_copy(weight_ref, weight_hbm.at[pl.ds(0, 16)])
-    copies[-1].wait()
     pltpu.sync_copy(tables, kept_hbm.at[pl.ds(0, TABLE_ROWS), :])
 
 
@@ -607,6 +648,7 @@
 
 
 def atoms_kernel(
+    first_step,
     frac_hbm,
     base_hbm,
     table_hbm,
@@ -620,47 +662,39 @@
     wz_ref,
     sems,
 ):
-    step = pl.program_id(0)
-
-    @pl.when(step == 0)
+    step = pl.program_id(0) + first_step
+
+    @pl.when(step == first_step)
     def _first():
         moves = [(frac_hbm, frac_ref), (base_hbm, base_ref), (table_hbm, table_ref)]
         for copy in start_all(moves, sems):
             copy.wait()
         prepare(frac_ref, base_ref, wx_ref, wy_ref, wz_ref, lambda chunk, rows: None)
 
-    def pair_step(index, carry):
-        cell = step * 16 + index * 2
-        high, low = pair_depth(base_ref, wz_ref, cell)
+    for index in range(8):
+        high, low = pair_depth(base_ref, wz_ref, step, index)
         both = dot(table_ref[...], high)
         depth_ref[index, 0], depth_ref[index, 1] = split(
             both[:256] + both[256:] + dot(table_ref[:256], low)
         )
-        window_out[index, pl.ds(8, 16), :] = pair_window_y(base_ref, wy_ref, cell)
+        window_out[index, pl.ds(8, 16), :] = pair_window_y(base_ref, wy_ref, step, index)
         for u in range(8):
-            window_out[index, pl.ds(u, 1), :] = pair_row(wx_ref, u, cell)
-        return carry
-
-    lax.fori_loop(0, 8, pair_step, 0, unroll=2)
+            window_out[index, pl.ds(u, 1), :] = pair_row(wx_ref, u, step, index)
 
 
 def gather_kernel(
     count_hbm,
     in_ref,
-    depth_hbm,
-    window_hbm,
-    out_ref,
-    count_ref,
-    depth_ref,
-    window_ref,
-    ext_ref,
-    sems,
+    *refs,
 ):
-    moves = [(count_hbm, count_ref), (window_hbm.at[pl.ds(0, CELLS // 2)], window_ref)]
-    for row in range(8):
-        pairs = pl.ds(8 * row, 8)
-        moves.append((depth_hbm.at[pairs], depth_ref.at[pairs]))
+    depth_refs, window_refs = refs[:ATOM_PARTS], refs[ATOM_PARTS : 2 * ATOM_PARTS]
+    out_ref, count_ref, late_ref, ext_ref, sems = refs[2 * ATOM_PARTS :]
+    moves = [(count_hbm, count_ref)]
+    for row in range(4):
+        late = pl.ds(8 * row, 8)
+        moves.append((depth_refs[-1].at[late], late_ref.at[late]))
     copies = start_all(moves, sems)
+    depth_refs = (*depth_refs[:-1], late_ref)
 
     def turned(row):
         block = in_ref[pl.ds(row, 128, stride=ROWS), :].T
@@ -682,27 +716,30 @@
         first, second = turned(36 + rim)
         ext_ref.at[0][rows, :] = first[:EXT_X]
         ext_ref.at[1][rows, :] = second[:EXT_X]
-    for copy in copies[:2]:
-        copy.wait()
+    copies[0].wait()
 
     def pair_work(cell_x, pair):
         index = cell_x * 8 + pair
+        part = min(cell_x // 2, 2)
+        depth_ref, window_ref = depth_refs[part], window_refs[part]
+        inner = index - 16 * part
         windows = []
         for u in range(8):
             rows = pl.ds(pl.multiple_of((cell_x * 4 + u) * EXT_Y + pair * 8, 8), 16)
             windows.append(jnp.concatenate([ext_ref[0, rows, :], ext_ref[1, rows, :]], axis=1))
         high, low = split(jnp.concatenate(windows, axis=0))
-        both = dot(jnp.concatenate([high, low], axis=0), depth_ref[index, 0])
-        part = both[:128] + both[128:] + dot(high, depth_ref[index, 1])
-        total = part[:16] * window_ref[index, pl.ds(0, 1), :]
+        both = dot(jnp.concatenate([high, low], axis=0), depth_ref[inner, 0])
+        patch = both[:128] + both[128:] + dot(high, depth_ref[inner, 1])
+        total = patch[:16] * window_ref[inner, pl.ds(0, 1), :]
         for u in range(1, 8):
-            total += part[16 * u : 16 * u + 16] * window_ref[index, pl.ds(u, 1), :]
-        total = jnp.sum(total * window_ref[index, pl.ds(8, 16), :], axis=0, keepdims=True)
+            total += patch[16 * u : 16 * u + 16] * window_ref[inner, pl.ds(u, 1), :]
+        total = jnp.sum(total * window_ref[inner, pl.ds(8, 16), :], axis=0, keepdims=True)
         out_ref[pl.ds(index * 2, 1), :] = total[:, :128]
         out_ref[pl.ds(index * 2 + 1, 1), :] = total[:, 128:]
 
     for cell_x in range(8):
-        copies[2 + cell_x].wait()
+        if cell_x >= 4:
+            copies[cell_x - 3].wait()
         for pair in range(8):
             pair_work(cell_x, pair)
 
@@ -744,7 +781,7 @@
 def per_device(cotangent, fraction, grid_base, cell_count, influence):
     device = lax.axis_index("px") * PY + lax.axis_index("py")
     flags = jnp.stack([(device < MIDDLE).astype(jnp.int32), (device == MIDDLE).astype(jnp.int32)])
-    zero_plane = lax.ppermute(influence[0], ("px", "py"), [(0, MIDDLE)])
+    zero_plane = lax.ppermute(influence[0, :HALF_ROWS], ("px", "py"), [(0, MIDDLE)])
     fraction = fraction.reshape(ATOMS)
     grid_base = grid_base.reshape(ATOMS)
     forward_z, inverse_z = depth_tables()
@@ -800,31 +837,35 @@
     )(flags, influence, zero_plane, sort_table(), plane_tables())
 
     pairs = CELLS // 2
-    depth, window = pl.pallas_call(
-        atoms_kernel,
-        grid=(8,),
-        out_shape=(
-            jax.ShapeDtypeStruct((pairs, 2, 256, 256), BF),
-            jax.ShapeDtypeStruct((704, 24, 256), F32),
-        ),
-        in_specs=[HBM] * 3,
-        out_specs=(
-            pl.BlockSpec((8, 2, 256, 256), lambda i: (i, 0, 0, 0)),
-            pl.BlockSpec((8, 24, 256), lambda i: (i, 0, 0)),
-        ),
-        scratch_shapes=[
-            scratch(ATOMS),
-            scratch(ATOMS, jnp.int32),
-            scratch((512, 256), BF),
-            *WEIGHTS,
-            dmas(3),
-        ],
-        compiler_params=params(56),
-        cost_estimate=cost(10**10),
-        name="atoms",
-    )(fraction, grid_base, inverse_z)
-
-    planes, depth, window = lax.optimization_barrier((planes, depth, window))
+    depths, windows = [], []
+    for first_step, steps, room in ATOM_CALLS:
+        depth, window = pl.pallas_call(
+            functools.partial(atoms_kernel, first_step),
+            grid=(steps,),
+            out_shape=(
+                jax.ShapeDtypeStruct((room, 2, 256, 256), BF),
+                jax.ShapeDtypeStruct((8 * steps, 24, 256), F32),
+            ),
+            in_specs=[HBM] * 3,
+            out_specs=(
+                pl.BlockSpec((8, 2, 256, 256), lambda i: (i, 0, 0, 0)),
+                pl.BlockSpec((8, 24, 256), lambda i: (i, 0, 0)),
+            ),
+            scratch_shapes=[
+                scratch(ATOMS),
+                scratch(ATOMS, jnp.int32),
+                scratch((512, 256), BF),
+                *WEIGHTS,
+                dmas(3),
+            ],
+            compiler_params=params(60),
+            cost_estimate=cost(3 * 10**9),
+            name="atoms",
+        )(fraction, grid_base, inverse_z)
+        depths.append(depth)
+        windows.append(window)
+
+    planes, depths, windows = lax.optimization_barrier((planes, depths, windows))
     back = pl.pallas_call(
         plane_kernel,
         out_shape=jax.ShapeDtypeStruct((DEVICES * ROWS, 128), F32),
@@ -849,18 +890,17 @@
     gradient = pl.pallas_call(
         gather_kernel,
         out_shape=jax.ShapeDtypeStruct((CELLS, 128), F32),
-        in_specs=[HBM, VMEM, HBM, HBM],
+        in_specs=[HBM] + [VMEM] * ATOM_PARTS + [HBM] + [VMEM] * ATOM_PARTS,
         out_specs=VMEM,
         scratch_shapes=[
             pltpu.SMEM((8, 16), jnp.int32),
-            scratch((pairs, 2, 256, 256), BF),
-            scratch((pairs, 24, 256)),
+            scratch((pairs // 2, 2, 256, 256), BF),
             EXTENDED,
-            dmas(10),
+            dmas(5),
         ],
-        compiler_params=params(48),
+        compiler_params=params(40),
         name="gather",
-    )(cell_count, returned, depth, window)
+    )(cell_count, returned, *depths, *windows)
     return gradient.reshape(cotangent.shape)
 
 

time: 123 us -> 119 us (0.967)
  waiting for transfers between devices: 10.8 us -> 8.94 us
    all_to_all x1, waiting for transfers between devices: 10.8 us -> 8.94 us  [exchange(): lax.all_to_all(array, ('px', 'py'), split_axis=0, concat_axis=0, tiled=True)]
    pallas_call x1, Pallas kernels: 7.98 us -> 6.47 us  [per_device(): pl.pallas_call(gather_kernel, out_shape=jax.ShapeDtypeStruct((CELLS, 128)...]
    pallas_call x1 -> x3, Pallas kernels: 17.9 us -> 18.6 us  [per_device(): pl.pallas_call(functools.partial(atoms_kernel, first_step), grid=(steps,)...]
  transfers between devices with their start and end apart: 2 -> 2, of which waited for: 1 -> 1; matrix products, arithmetic and copies ran while one was open for 0% -> 1% of each run, Pallas kernels for 30% -> 31%
where the time goes in v3:
time: 119 us
  Pallas kernels  55.5 us (47%)
  blocking collectives  40.3 us (34%)
  starting transfers between devices  11.8 us (10%)
  waiting for transfers between devices  8.94 us (8%)
    all_to_all x1, blocking collectives, exchange(): lax.all_to_all(array, ('px', 'py'), split_axis=0, concat_axis=0, tiled=True)  40.3 us
    pallas_call x3, Pallas kernels, per_device(): pl.pallas_call(functools.partial(atoms_kernel, first_step), grid=(steps,)...  18.6 us
    pallas_call x1, Pallas kernels, per_device(): pl.pallas_call(plane_kernel, out_shape=jax.ShapeDtypeStruct((DEVICES * RO...  12 us
    pallas_call x1, Pallas kernels, per_device(): pl.pallas_call(spread_kernel, out_shape=jax.ShapeDtypeStruct((DEVICES, RO...  11.2 us
    all_to_all x1, waiting for transfers between devices, exchange(): lax.all_to_all(array, ('px', 'py'), split_axis=0, concat_axis=0, tiled=True)  8.94 us
    pallas_call x1, Pallas kernels, per_device(): pl.pallas_call(sort_kernel, out_shape=(jax.ShapeDtypeStruct((136, 256, 12...  7.37 us
    pallas_call x1, Pallas kernels, per_device(): pl.pallas_call(gather_kernel, out_shape=jax.ShapeDtypeStruct((CELLS, 128)...  6.47 us
    all_to_all x1, starting transfers between devices, exchange(): lax.all_to_all(array, ('px', 'py'), split_axis=0, concat_axis=0, tiled=True)  5.95 us
  transfers between devices with their start and end apart: 2, of which 1 were waited for; matrix products, arithmetic and copies ran while one was open for 1% of the time, Pallas kernels for 31%

profile of v3, /device:TPU:0, one launch (start us, length us, event | category | flops | bytes accessed | tf_op | source)
XLA Modules:
  0.0 118.8 jit_solution(7365186522624857367)
XLA Ops:
  0.0 1.1 slice_bitcast_fusion
  1.1 5.9 %collective-permute-start = (f32[264,512]{1,0:T(8,128)S(1)}, f32[264,512]{1,0:T(8,128)S(1)}, u32[]{:S(2)}, u32[]{:S(2)}) collective-permute-start(f32[264,512]{1,0:T(8,128)S(1)} %slice_bitcast_fusion), channel_id=1, source_target_pairs={{0,64}} | collective-permute-start | bytes 1622024 | tf_op jit(solution)/shard_map/ppermute | solution.py:784
  7.0 11.2 %spread.1 = f32[128,40,128]{2,1,0:T(8,128)} custom-call(s32[8,16]{1,0:T(8,128)} %count_hbm.3, f32[128,128]{1,0:T(8,128)} %bitcast.22, f32[3,128,128]{2,1,0:T(8,128)} %bitcast.14, s32[3,128,128]{2,1,0:T(8,128)} %bitcast.18, bf16[512,256]{1,0:T(8,128)(2,1)} %constant.21.clone.table_hbm), custom_call_target="tpu_custom_call" | custom-call | flops 10000000000 | bytes 10000000 | tf_op jit(solution)/shard_map/spread/pallas_call | solution.py:789
  18.2 0.0 collective-permute-done.zero_hbm
  18.2 0.0 copy-start.7
  18.2 5.9 %all-to-all-start = ((f32[128,40,128]{2,1,0:T(8,128)}), f32[128,40,128]{2,1,0:T(8,128)S(1)}, u32[]{:S(2)}, u32[]{:S(2)}) async-start(f32[128,40,128]{2,1,0:T(8,128)} %spread.1), calls=%async_computation | async-start | bytes 5242880 | tf_op jit(solution)/shard_map/all_to_all | solution.py:812
  24.1 0.7 add_convert_fusion.flag_ref
  24.8 0.0 copy-done.7
  24.8 7.4 %sort_influence.1 = (f32[136,256,128]{2,1,0:T(8,128)}, bf16[34816,256]{1,0:T(8,128)(2,1)}) custom-call(s32[2]{0:T(128)} %add_convert_fusion.flag_ref, f32[2,512,512]{2,1,0:T(8,128)} %influence_hbm.1, f32[264,512]{1,0:T(8,128)} %copy-done.7, bf16[512,512]{1,0:T(8,128)(2,1)} %constant.22.clone.sort_hbm, bf16[7168,256]{1,0:T(8,128)(2,1)} %constant.23.clone.tables_hbm), custom_call_target="tpu_custom_call" | custom-call | flops 1000000000 | bytes 10000000 | tf_op jit(solution)/shard_map/sort_influence/pallas_call | solution.py:818
  32.2 5.3 %atoms.4 = (bf16[16,2,256,256]{3,2,1,0:T(8,128)(2,1)}, f32[16,24,256]{2,1,0:T(8,128)}) custom-call(f32[3,128,128]{2,1,0:T(8,128)} %bitcast.15, s32[3,128,128]{2,1,0:T(8,128)} %bitcast.19, bf16[512,256]{1,0:T(8,128)(2,1)} %constant.24.clone.table_hbm), custom_call_target="tpu_custom_call" | custom-call | flops 3000000000 | bytes 10000000 | tf_op jit(solution)/shard_map/atoms/pallas_call | solution.py:842
  37.5 5.4 %atoms.3 = (bf16[16,2,256,256]{3,2,1,0:T(8,128)(2,1)}, f32[16,24,256]{2,1,0:T(8,128)}) custom-call(f32[3,128,128]{2,1,0:T(8,128)} %bitcast.16, s32[3,128,128]{2,1,0:T(8,128)} %bitcast.20, bf16[512,256]{1,0:T(8,128)(2,1)} %constant.24.clone.table_hbm), custom_call_target="tpu_custom_call" | custom-call | flops 3000000000 | bytes 10000000 | tf_op jit(solution)/shard_map/atoms/pallas_call | solution.py:842
  42.9 0.0 copy-start.6
  42.9 7.8 %atoms.5 = (bf16[80,2,256,256]{3,2,1,0:T(8,128)(2,1)}, f32[32,24,256]{2,1,0:T(8,128)}) custom-call(f32[3,128,128]{2,1,0:T(8,128)} %bitcast.17, s32[3,128,128]{2,1,0:T(8,128)} %bitcast.21, bf16[512,256]{1,0:T(8,128)(2,1)} %constant.24.clone.table_hbm), custom_call_target="tpu_custom_call" | custom-call | flops 3000000000 | bytes 10000000 | tf_op jit(solution)/shard_map/atoms/pallas_call | solution.py:842
  50.8 8.9 %all-to-all-done = f32[128,40,128]{2,1,0:T(8,128)S(1)} async-done(((f32[128,40,128]{2,1,0:T(8,128)}), f32[128,40,128]{2,1,0:T(8,128)S(1)}, u32[]{:S(2)}, u32[]{:S(2)}) %all-to-all-start) | async-done | bytes 2621472 | tf_op jit(solution)/shard_map/all_to_all | solution.py:812
  59.7 0.0 copy-done.6
  59.7 0.0 copy-start.1
  59.7 0.0 copy-start.3
  59.7 0.0 copy-start.4
  59.7 12.0 %planes.1 = f32[5120,128]{1,0:T(8,128)S(1)} custom-call(s32[2]{0:T(128)S(1)} %copy-done.6, f32[5120,128]{1,0:T(8,128)S(1)} %bitcast.12, f32[136,256,128]{2,1,0:T(8,128)} %get-tuple-element.35.weight_hbm, bf16[34816,256]{1,0:T(8,128)(2,1)} %get-tuple-element.36.tables_hbm), custom_call_target="tpu_custom_call" | custom-call | tf_op jit(solution)/shard_map/planes/pallas_call | solution.py:869
  71.7 0.0 copy-start
  71.7 0.0 copy-start.2
  71.7 0.0 copy-start.5
  71.7 40.3 %all_to_all.10 = f32[128,40,128]{2,1,0:T(8,128)S(1)} all-to-all(f32[128,40,128]{2,1,0:T(8,128)S(1)} %bitcast.13), channel_id=1, replica_groups=mesh['px'=16,'py'=8] {'px','py'}, dimensions={0} | all-to-all | bytes 5242880 | tf_op jit(solution)/shard_map/all_to_all | solution.py:812
  112.1 0.0 copy-done.1
  112.1 0.0 copy-done.3
  112.1 0.0 copy-done.4
  112.1 0.0 copy-done
  112.1 0.0 copy-done.2
  112.1 0.0 copy-done.5
  112.1 6.5 %gather.1 = f32[128,128]{1,0:T(8,128)} custom-call(s32[8,16]{1,0:T(8,128)S(1)} %copy-done.5, f32[5120,128]{1,0:T(8,128)S(1)} %bitcast.11, bf16[16,2,256,256]{3,2,1,0:T(8,128)(2,1)S(1)} %copy-done.1, bf16[16,2,256,256]{3,2,1,0:T(8,128)(2,1)S(1)} %copy-done, bf16[80,2,256,256]{3,2,1,0:T(8,128)(2,1)} %get-tuple-element.39.refs_2_, ...), custom_call_target="tpu_custom_call" | custom-call | tf_op jit(solution)/shard_map/gather/pallas_call | solution.py:890
Async XLA Ops:
  1.1 17.1 %collective-permute-start = (f32[264,512]{1,0:T(8,128)S(1)}, f32[264,512]{1,0:T(8,128)S(1)}, u32[]{:S(2)}, u32[]{:S(2)}) collective-permute-start(f32[264,512]{1,0:T(8,128)S(1)} %slice_bitcast_fusion), channel_id=1, source_target_pairs={{0,64}} | collective-permute-start | bytes 1622024 | tf_op jit(solution)/shard_map/ppermute | solution.py:784
  18.2 6.6 %copy-start.7 = (f32[264,512]{1,0:T(8,128)}, f32[264,512]{1,0:T(8,128)S(1)}, u32[]{:S(2)}) copy-start(f32[264,512]{1,0:T(8,128)S(1)} %collective-permute-done.zero_hbm) | copy-start | bytes 1622020
  18.2 41.5 %all-to-all-start = ((f32[128,40,128]{2,1,0:T(8,128)}), f32[128,40,128]{2,1,0:T(8,128)S(1)}, u32[]{:S(2)}, u32[]{:S(2)}) async-start(f32[128,40,128]{2,1,0:T(8,128)} %spread.1), calls=%async_computation | async-start | bytes 5242880 | tf_op jit(solution)/shard_map/all_to_all | solution.py:812
  42.9 16.8 %copy-start.6 = (s32[2]{0:T(128)S(1)}, s32[2]{0:T(128)}, u32[]{:S(2)}) copy-start(s32[2]{0:T(128)} %add_convert_fusion.flag_ref) | copy-start | bytes 28
  59.7 52.4 %copy-start.1 = (bf16[16,2,256,256]{3,2,1,0:T(8,128)(2,1)S(1)}, bf16[16,2,256,256]{3,2,1,0:T(8,128)(2,1)}, u32[]{:S(2)}) copy-start(bf16[16,2,256,256]{3,2,1,0:T(8,128)(2,1)} %get-tuple-element.37.refs_0_) | copy-start | bytes 12582916
  59.7 52.4 %copy-start.3 = (f32[16,24,256]{2,1,0:T(8,128)S(1)}, f32[16,24,256]{2,1,0:T(8,128)}, u32[]{:S(2)}) copy-start(f32[16,24,256]{2,1,0:T(8,128)} %get-tuple-element.41.refs_4_) | copy-start | bytes 1179652
  59.7 52.4 %copy-start.4 = (f32[16,24,256]{2,1,0:T(8,128)S(1)}, f32[16,24,256]{2,1,0:T(8,128)}, u32[]{:S(2)}) copy-start(f32[16,24,256]{2,1,0:T(8,128)} %get-tuple-element.40.refs_3_) | copy-start | bytes 1179652
  71.7 40.4 %copy-start = (bf16[16,2,256,256]{3,2,1,0:T(8,128)(2,1)S(1)}, bf16[16,2,256,256]{3,2,1,0:T(8,128)(2,1)}, u32[]{:S(2)}) copy-start(bf16[16,2,256,256]{3,2,1,0:T(8,128)(2,1)} %get-tuple-element.38.refs_1_) | copy-start | bytes 12582916
  71.7 40.4 %copy-start.2 = (f32[32,24,256]{2,1,0:T(8,128)S(1)}, f32[32,24,256]{2,1,0:T(8,128)}, u32[]{:S(2)}) copy-start(f32[32,24,256]{2,1,0:T(8,128)} %get-tuple-element.42.refs_5_) | copy-start | bytes 2359300
  71.7 40.4 %copy-start.5 = (s32[8,16]{1,0:T(8,128)S(1)}, s32[8,16]{1,0:T(8,128)}, u32[]{:S(2)}) copy-start(s32[8,16]{1,0:T(8,128)} %count_hbm.3) | copy-start | bytes 1540

commit v4 on v3

--- a/solution.py
+++ b/solution.py
@@ -165,7 +165,7 @@
             wz_ref[degree, rows, :] = weight
         return carry
 
-    lax.fori_loop(0, CELLS // 8, chunk_step, 0)
+    lax.fori_loop(0, CELLS // 8, chunk_step, 0, unroll=4)
 
 
 def cell_rows(ref, index, cell_x, cell_y):
@@ -450,21 +450,22 @@
 
     moves = [
         table_move(0, Y_ROWS),
-        table_move(X_START, X_ROWS),
+        table_move(X_START, 2048),
         (weight_hbm.at[pl.ds(0, 8)], weight_ref.at[pl.ds(0, 8)]),
         table_move(TURN_START, TURN_ROWS),
         (weight_hbm.at[pl.ds(8, 8)], weight_ref.at[pl.ds(8, 8)]),
+        table_move(X_START + 2048, 1024),
     ]
     copies = [
         pltpu.make_async_copy(source, target, sems.at[index])
         for index, (source, target) in enumerate(moves)
     ]
-    for copy in copies[:3]:
+    for copy in (*copies[:3], copies[5]):
         copy.start()
 
     @pl.when(middle != 0)
     def _more():
-        for copy in copies[3:]:
+        for copy in copies[3:5]:
             copy.start()
 
     sub = lax.broadcasted_iota(jnp.int32, (8, 128), 0)
@@ -541,18 +542,20 @@
 
     blocks = [(f, residue) for f in (0, 1) for residue in range(4)]
     copies[0].wait()
-    copies[1].wait()
     for f, residue in blocks:
         which = 4 * f + residue
         high = jnp.concatenate([block_high[which], rim_high[f]], axis=1)
         low = jnp.concatenate([block_low[which], rim_low[f]], axis=1)
         both = dot(jnp.concatenate([high, low], axis=0), y_table(residue, 0))
         along_y = both[:256] + both[256:] + dot(high, y_table(residue, 1))
+        if which == 0:
+            copies[1].wait()
         cosine, sine = left_products(x_table(f), along_y)
         spectrum[which, :, :128] = cosine[:, :128] + sine[:, 128:]
         spectrum[which, :, 128:] = cosine[:, 128:] - sine[:, :128]
 
     copies[2].wait()
+    copies[5].wait()
 
     @pl.when(middle == 0)
     def _scale():
@@ -880,7 +883,7 @@
             scratch((2, 256, 128), BF),
             scratch((8, 256, 256)),
             scratch((8, 256, 384)),
-            dmas(5),
+            dmas(6),
         ],
         compiler_params=params(48),
         name="planes",

time: 119 us -> 119 us (level)
  no operation moved by 1% of the time
where the time goes in v4:
time: 119 us; the launch traced here: 118 us
  Pallas kernels  54.7 us (46%)
  blocking collectives  40.3 us (34%)
  starting transfers between devices  11.8 us (10%)
  waiting for transfers between devices  8.95 us (8%)
    all_to_all x1, blocking collectives, exchange(): lax.all_to_all(array, ('px', 'py'), split_axis=0, concat_axis=0, tiled=True)  40.3 us
    pallas_call x3, Pallas kernels, per_device(): pl.pallas_call(functools.partial(atoms_kernel, first_step), grid=(steps,)...  18.4 us
    pallas_call x1, Pallas kernels, per_device(): pl.pallas_call(plane_kernel, out_shape=jax.ShapeDtypeStruct((DEVICES * RO...  11.2 us
    pallas_call x1, Pallas kernels, per_device(): pl.pallas_call(spread_kernel, out_shape=jax.ShapeDtypeStruct((DEVICES, RO...  11.1 us
    all_to_all x1, waiting for transfers between devices, exchange(): lax.all_to_all(array, ('px', 'py'), split_axis=0, concat_axis=0, tiled=True)  8.95 us
    pallas_call x1, Pallas kernels, per_device(): pl.pallas_call(sort_kernel, out_shape=(jax.ShapeDtypeStruct((136, 256, 12...  7.54 us
    pallas_call x1, Pallas kernels, per_device(): pl.pallas_call(gather_kernel, out_shape=jax.ShapeDtypeStruct((CELLS, 128)...  6.46 us
    all_to_all x1, starting transfers between devices, exchange(): lax.all_to_all(array, ('px', 'py'), split_axis=0, concat_axis=0, tiled=True)  5.95 us
  transfers between devices with their start and end apart: 2, of which 1 were waited for; matrix products, arithmetic and copies ran while one was open for 1% of the time, Pallas kernels for 31%

profile of v4, /device:TPU:0, one launch (start us, length us, event | category | flops | bytes accessed | tf_op | source)
XLA Modules:
  0.0 118.0 jit_solution(13215085526940212974)
XLA Ops:
  0.0 1.1 slice_bitcast_fusion
  1.1 5.9 %collective-permute-start = (f32[264,512]{1,0:T(8,128)S(1)}, f32[264,512]{1,0:T(8,128)S(1)}, u32[]{:S(2)}, u32[]{:S(2)}) collective-permute-start(f32[264,512]{1,0:T(8,128)S(1)} %slice_bitcast_fusion), channel_id=1, source_target_pairs={{0,64}} | collective-permute-start | bytes 1622024 | tf_op jit(solution)/shard_map/ppermute | solution.py:787
  7.0 11.1 %spread.1 = f32[128,40,128]{2,1,0:T(8,128)} custom-call(s32[8,16]{1,0:T(8,128)} %count_hbm.3, f32[128,128]{1,0:T(8,128)} %bitcast.22, f32[3,128,128]{2,1,0:T(8,128)} %bitcast.14, s32[3,128,128]{2,1,0:T(8,128)} %bitcast.18, bf16[512,256]{1,0:T(8,128)(2,1)} %constant.21.clone.table_hbm), custom_call_target="tpu_custom_call" | custom-call | flops 10000000000 | bytes 10000000 | tf_op jit(solution)/shard_map/spread/pallas_call | solution.py:792
  18.1 0.0 collective-permute-done.zero_hbm
  18.1 0.0 copy-start.7
  18.1 5.9 %all-to-all-start = ((f32[128,40,128]{2,1,0:T(8,128)}), f32[128,40,128]{2,1,0:T(8,128)S(1)}, u32[]{:S(2)}, u32[]{:S(2)}) async-start(f32[128,40,128]{2,1,0:T(8,128)} %spread.1), calls=%async_computation | async-start | bytes 5242880 | tf_op jit(solution)/shard_map/all_to_all | solution.py:815
  24.0 0.7 add_convert_fusion.flag_ref
  24.7 0.0 copy-done.7
  24.7 7.5 %sort_influence.1 = (f32[136,256,128]{2,1,0:T(8,128)}, bf16[34816,256]{1,0:T(8,128)(2,1)}) custom-call(s32[2]{0:T(128)} %add_convert_fusion.flag_ref, f32[2,512,512]{2,1,0:T(8,128)} %influence_hbm.1, f32[264,512]{1,0:T(8,128)} %copy-done.7, bf16[512,512]{1,0:T(8,128)(2,1)} %constant.22.clone.sort_hbm, bf16[7168,256]{1,0:T(8,128)(2,1)} %constant.23.clone.tables_hbm), custom_call_target="tpu_custom_call" | custom-call | flops 1000000000 | bytes 10000000 | tf_op jit(solution)/shard_map/sort_influence/pallas_call | solution.py:821
  32.3 5.3 %atoms.4 = (bf16[16,2,256,256]{3,2,1,0:T(8,128)(2,1)}, f32[16,24,256]{2,1,0:T(8,128)}) custom-call(f32[3,128,128]{2,1,0:T(8,128)} %bitcast.15, s32[3,128,128]{2,1,0:T(8,128)} %bitcast.19, bf16[512,256]{1,0:T(8,128)(2,1)} %constant.24.clone.table_hbm), custom_call_target="tpu_custom_call" | custom-call | flops 3000000000 | bytes 10000000 | tf_op jit(solution)/shard_map/atoms/pallas_call | solution.py:845
  37.5 5.3 %atoms.3 = (bf16[16,2,256,256]{3,2,1,0:T(8,128)(2,1)}, f32[16,24,256]{2,1,0:T(8,128)}) custom-call(f32[3,128,128]{2,1,0:T(8,128)} %bitcast.16, s32[3,128,128]{2,1,0:T(8,128)} %bitcast.20, bf16[512,256]{1,0:T(8,128)(2,1)} %constant.24.clone.table_hbm), custom_call_target="tpu_custom_call" | custom-call | flops 3000000000 | bytes 10000000 | tf_op jit(solution)/shard_map/atoms/pallas_call | solution.py:845
  42.9 0.0 copy-start.6
  42.9 7.8 %atoms.5 = (bf16[80,2,256,256]{3,2,1,0:T(8,128)(2,1)}, f32[32,24,256]{2,1,0:T(8,128)}) custom-call(f32[3,128,128]{2,1,0:T(8,128)} %bitcast.17, s32[3,128,128]{2,1,0:T(8,128)} %bitcast.21, bf16[512,256]{1,0:T(8,128)(2,1)} %constant.24.clone.table_hbm), custom_call_target="tpu_custom_call" | custom-call | flops 3000000000 | bytes 10000000 | tf_op jit(solution)/shard_map/atoms/pallas_call | solution.py:845
  50.7 9.0 %all-to-all-done = f32[128,40,128]{2,1,0:T(8,128)S(1)} async-done(((f32[128,40,128]{2,1,0:T(8,128)}), f32[128,40,128]{2,1,0:T(8,128)S(1)}, u32[]{:S(2)}, u32[]{:S(2)}) %all-to-all-start) | async-done | bytes 2621472 | tf_op jit(solution)/shard_map/all_to_all | solution.py:815
  59.6 0.0 copy-done.6
  59.6 0.0 copy-start.1
  59.6 0.0 copy-start.3
  59.6 0.0 copy-start.4
  59.6 11.2 %planes.1 = f32[5120,128]{1,0:T(8,128)S(1)} custom-call(s32[2]{0:T(128)S(1)} %copy-done.6, f32[5120,128]{1,0:T(8,128)S(1)} %bitcast.12, f32[136,256,128]{2,1,0:T(8,128)} %get-tuple-element.35.weight_hbm, bf16[34816,256]{1,0:T(8,128)(2,1)} %get-tuple-element.36.tables_hbm), custom_call_target="tpu_custom_call" | custom-call | tf_op jit(solution)/shard_map/planes/pallas_call | solution.py:872
  70.9 0.0 copy-start
  70.9 0.0 copy-start.2
  70.9 0.0 copy-start.5
  70.9 40.3 %all_to_all.10 = f32[128,40,128]{2,1,0:T(8,128)S(1)} all-to-all(f32[128,40,128]{2,1,0:T(8,128)S(1)} %bitcast.13), channel_id=1, replica_groups=mesh['px'=16,'py'=8] {'px','py'}, dimensions={0} | all-to-all | bytes 5242880 | tf_op jit(solution)/shard_map/all_to_all | solution.py:815
  111.3 0.0 copy-done.1
  111.3 0.0 copy-done.3
  111.3 0.0 copy-done.4
  111.3 0.0 copy-done
  111.3 0.0 copy-done.2
  111.3 0.0 copy-done.5
  111.3 6.5 %gather.1 = f32[128,128]{1,0:T(8,128)} custom-call(s32[8,16]{1,0:T(8,128)S(1)} %copy-done.5, f32[5120,128]{1,0:T(8,128)S(1)} %bitcast.11, bf16[16,2,256,256]{3,2,1,0:T(8,128)(2,1)S(1)} %copy-done.1, bf16[16,2,256,256]{3,2,1,0:T(8,128)(2,1)S(1)} %copy-done, bf16[80,2,256,256]{3,2,1,0:T(8,128)(2,1)} %get-tuple-element.39.refs_2_, ...), custom_call_target="tpu_custom_call" | custom-call | tf_op jit(solution)/shard_map/gather/pallas_call | solution.py:893
Async XLA Ops:
  1.1 17.0 %collective-permute-start = (f32[264,512]{1,0:T(8,128)S(1)}, f32[264,512]{1,0:T(8,128)S(1)}, u32[]{:S(2)}, u32[]{:S(2)}) collective-permute-start(f32[264,512]{1,0:T(8,128)S(1)} %slice_bitcast_fusion), channel_id=1, source_target_pairs={{0,64}} | collective-permute-start | bytes 1622024 | tf_op jit(solution)/shard_map/ppermute | solution.py:787
  18.1 6.6 %copy-start.7 = (f32[264,512]{1,0:T(8,128)}, f32[264,512]{1,0:T(8,128)S(1)}, u32[]{:S(2)}) copy-start(f32[264,512]{1,0:T(8,128)S(1)} %collective-permute-done.zero_hbm) | copy-start | bytes 1622020
  18.1 41.5 %all-to-all-start = ((f32[128,40,128]{2,1,0:T(8,128)}), f32[128,40,128]{2,1,0:T(8,128)S(1)}, u32[]{:S(2)}, u32[]{:S(2)}) async-start(f32[128,40,128]{2,1,0:T(8,128)} %spread.1), calls=%async_computation | async-start | bytes 5242880 | tf_op jit(solution)/shard_map/all_to_all | solution.py:815
  42.9 16.8 %copy-start.6 = (s32[2]{0:T(128)S(1)}, s32[2]{0:T(128)}, u32[]{:S(2)}) copy-start(s32[2]{0:T(128)} %add_convert_fusion.flag_ref) | copy-start | bytes 28
  59.6 51.6 %copy-start.1 = (bf16[16,2,256,256]{3,2,1,0:T(8,128)(2,1)S(1)}, bf16[16,2,256,256]{3,2,1,0:T(8,128)(2,1)}, u32[]{:S(2)}) copy-start(bf16[16,2,256,256]{3,2,1,0:T(8,128)(2,1)} %get-tuple-element.37.refs_0_) | copy-start | bytes 12582916
  59.6 51.6 %copy-start.3 = (f32[16,24,256]{2,1,0:T(8,128)S(1)}, f32[16,24,256]{2,1,0:T(8,128)}, u32[]{:S(2)}) copy-start(f32[16,24,256]{2,1,0:T(8,128)} %get-tuple-element.41.refs_4_) | copy-start | bytes 1179652
  59.6 51.6 %copy-start.4 = (f32[16,24,256]{2,1,0:T(8,128)S(1)}, f32[16,24,256]{2,1,0:T(8,128)}, u32[]{:S(2)}) copy-start(f32[16,24,256]{2,1,0:T(8,128)} %get-tuple-element.40.refs_3_) | copy-start | bytes 1179652
  70.9 40.4 %copy-start = (bf16[16,2,256,256]{3,2,1,0:T(8,128)(2,1)S(1)}, bf16[16,2,256,256]{3,2,1,0:T(8,128)(2,1)}, u32[]{:S(2)}) copy-start(bf16[16,2,256,256]{3,2,1,0:T(8,128)(2,1)} %get-tuple-element.38.refs_1_) | copy-start | bytes 12582916
  70.9 40.4 %copy-start.2 = (f32[32,24,256]{2,1,0:T(8,128)S(1)}, f32[32,24,256]{2,1,0:T(8,128)}, u32[]{:S(2)}) copy-start(f32[32,24,256]{2,1,0:T(8,128)} %get-tuple-element.42.refs_5_) | copy-start | bytes 2359300
  70.9 40.4 %copy-start.5 = (s32[8,16]{1,0:T(8,128)S(1)}, s32[8,16]{1,0:T(8,128)}, u32[]{:S(2)}) copy-start(s32[8,16]{1,0:T(8,128)} %count_hbm.3) | copy-start | bytes 1540
